TPU v7x, 128 devices: a whole 4x4x4 slice. The times are simulated.
128 devices in a mesh: dp: 16 (over y_lo, x, core), feat: 8 (over z, y_hi).
Axes of the slice: x: 4, y: 4 (y_hi: 2, y_lo: 2; y = y_hi * 2 + y_lo), z: 4, core: 2. Of those that a mesh axis runs over, the one named last changes fastest.
Arguments:
- activations: bfloat16 [16384, 8192], P('dp', 'feat'), may hold values from -6 to 6
- gradients: bfloat16 [16384, 8192], P('dp', 'feat'), may hold values from -6 to 6
- start_act: float32 [8192, 128], P('feat'), may hold values from -6 to 6
- start_grad: float32 [8192, 128], P('feat'), may hold values from -6 to 6
- doc_ids: int32 [16384], P('dp'), may hold values from 0 to 31, never falling along the last dimension, each value on 1 to 1024 neighbouring positions
Outputs:
- basis_act: float32 [8192, 128], P('feat')
- basis_grad: float32 [8192, 128], P('feat')
- scales: float32 [128, 128], replicated
Inputs may be any that keep to these rules, and one draw needn't show every extreme that they name: `doc_ids`: each document's tokens are consecutive and in order of id; every id occurs, and some document has exactly 1024 tokens.
All inputs are finite; a program needn't handle non-finite values.
Results may differ from a plain program's by a relative error of at most 0.0003.
Values sent between devices are 32-bit elements; how exact they have to be, the bound alone decides.
A program may use at most 64 MiB of HBM per device.

v0:
```python
import jax
import jax.numpy as jnp
from jax import lax
from jax.sharding import PartitionSpec as P

ITERS = 6


highest = lax.Precision.HIGHEST


def gram_of(image):
    return lax.dot_general(image, image, (((0,), (0,)), ((), ())), precision=highest)


def orthonormal(image, gram_mat):
    lower = jnp.linalg.cholesky(gram_mat)
    return jax.scipy.linalg.solve_triangular(lower, image.T, lower=True).T


def tokens_contract(wide, projected):
    return lax.dot_general(wide, projected, (((0,), (0,)), ((), ())), precision=highest)


def local(activations, gradients, start_act, start_grad, doc_ids):
    act_wide = activations.astype(jnp.float32)
    grad_wide = gradients.astype(jnp.float32)

    def project(basis):
        return lax.psum(
            (
                jnp.dot(act_wide, basis[0], precision=highest),
                jnp.dot(grad_wide, basis[1], precision=highest),
            ),
            "feat",
        )

    basis = (start_act, start_grad)
    for sweep in range(ITERS):
        projected = project(basis)
        images = (tokens_contract(act_wide, projected[0]), tokens_contract(grad_wide, projected[1]))
        summed = lax.psum((images[0], images[1]), "dp")
        grams = lax.psum((gram_of(summed[0]), gram_of(summed[1])), "feat")
        basis = (orthonormal(summed[0], grams[0]), orthonormal(summed[1], grams[1]))
    proj_act, proj_grad = project(basis)
    documents = 2 * lax.axis_size("dp")
    onehot = (doc_ids[:, None] == jnp.arange(documents, dtype=jnp.int32)[None, :]).astype(
        jnp.float32
    )
    counts = lax.psum(jnp.sum(onehot, axis=0), "dp")
    weight = jnp.dot(onehot, 1.0 / (documents * counts), precision=highest)
    left = weight[:, None] * proj_grad * proj_grad
    partial_scales = tokens_contract(left, proj_act * proj_act)
    scales = lax.psum(partial_scales, "dp")
    return (basis[0], basis[1], scales)


def solution(mesh):
    placed = (P("dp", "feat"), P("dp", "feat"), P("feat", None), P("feat", None), P("dp"))
    return jax.shard_map(
        local,
        mesh=mesh,
        in_specs=placed,
        out_specs=(P("feat", None), P("feat", None), P()),
        check_vma=False,
    )
```

profile of v0, /device:TPU:1, one launch (start us, length us, event | category | flops | bytes accessed | tf_op | source)
XLA Modules:
  0.0 2375.5 jit_solution(1988035948887498043)
XLA Ops:
  7.2 4.4 fusion.80
  14.4 89.3 %all-reduce.78.cloned.1.call-done = (f32[1024,128]{1,0:T(8,128)}, f32[1024,128]{1,0:T(8,128)}) async-done(((f32[1024,128]{1,0:T(8,128)}, f32[1024,128]{1,0:T(8,128)}), (f32[1024,128]{1,0:T(8,128)}, f32[1024,128]{1,0:T(8,128)})) %all-reduce.78.cloned.1.call-update) | async-done | bytes 1048592 | tf_op jit(solution)/shard_map/psum | solution.py:30
  103.6 3.1 convolution_bitcast_fusion.12
  108.7 122.3 %all-reduce.52.cloned.1.call-done = (f32[1024,128]{0,1:T(8,128)}, f32[1024,128]{0,1:T(8,128)}) async-done(((f32[1024,128]{0,1:T(8,128)}, f32[1024,128]{0,1:T(8,128)}), (f32[1024,128]{0,1:T(8,128)}, f32[1024,128]{0,1:T(8,128)})) %all-reduce.52.cloned.1.call-update) | async-done | bytes 1048592 | tf_op jit(solution)/shard_map/psum | solution.py:42
  236.3 79.9 %all-reduce.76.cloned.1.call-done = (f32[128,128]{0,1:T(8,128)}, f32[128,128]{0,1:T(8,128)}) async-done(((f32[128,128]{0,1:T(8,128)}, f32[128,128]{0,1:T(8,128)}), (f32[128,128]{0,1:T(8,128)}, f32[128,128]{0,1:T(8,128)})) %all-reduce.76.cloned.1.call-update) | async-done | bytes 131088 | tf_op jit(solution)/shard_map/psum | solution.py:43
  318.9 11.7 cholesky.260
  332.0 9.8 custom-call.22
  342.4 3.0 convolution_bitcast_fusion.11
  345.4 11.7 cholesky.194
  358.5 10.3 custom-call.16
  369.4 4.6 convolution_bitcast_fusion.22
  374.1 88.9 %all-reduce.74.cloned.1.call-done = (f32[1024,128]{0,1:T(8,128)}, f32[1024,128]{0,1:T(8,128)}) async-done(((f32[1024,128]{0,1:T(8,128)}, f32[1024,128]{0,1:T(8,128)}), (f32[1024,128]{0,1:T(8,128)}, f32[1024,128]{0,1:T(8,128)})) %all-reduce.74.cloned.1.call-update) | async-done | bytes 1048592 | tf_op jit(solution)/shard_map/psum | solution.py:30
  462.9 3.0 convolution_bitcast_fusion.10
  467.8 122.4 %all-reduce.50.cloned.1.call-done = (f32[1024,128]{0,1:T(8,128)}, f32[1024,128]{0,1:T(8,128)}) async-done(((f32[1024,128]{0,1:T(8,128)}, f32[1024,128]{0,1:T(8,128)}), (f32[1024,128]{0,1:T(8,128)}, f32[1024,128]{0,1:T(8,128)})) %all-reduce.50.cloned.1.call-update) | async-done | bytes 1048592 | tf_op jit(solution)/shard_map/psum | solution.py:42
  595.4 80.0 %all-reduce.72.cloned.1.call-done = (f32[128,128]{0,1:T(8,128)}, f32[128,128]{0,1:T(8,128)}) async-done(((f32[128,128]{0,1:T(8,128)}, f32[128,128]{0,1:T(8,128)}), (f32[128,128]{0,1:T(8,128)}, f32[128,128]{0,1:T(8,128)})) %all-reduce.72.cloned.1.call-update) | async-done | bytes 131088 | tf_op jit(solution)/shard_map/psum | solution.py:43
  677.2 11.7 cholesky.271
  690.2 9.8 custom-call.23
  700.7 3.0 convolution_bitcast_fusion.9
  703.8 11.7 cholesky.205
  716.8 10.0 custom-call.17
  727.5 4.6 convolution_bitcast_fusion.20
  732.1 88.9 %all-reduce.70.cloned.1.call-done = (f32[1024,128]{0,1:T(8,128)}, f32[1024,128]{0,1:T(8,128)}) async-done(((f32[1024,128]{0,1:T(8,128)}, f32[1024,128]{0,1:T(8,128)}), (f32[1024,128]{0,1:T(8,128)}, f32[1024,128]{0,1:T(8,128)})) %all-reduce.70.cloned.1.call-update) | async-done | bytes 1048592 | tf_op jit(solution)/shard_map/psum | solution.py:30
  821.0 3.6 convolution_bitcast_fusion.19
  826.5 122.4 %all-reduce.48.cloned.1.call-done = (f32[1024,128]{0,1:T(8,128)}, f32[1024,128]{0,1:T(8,128)}) async-done(((f32[1024,128]{0,1:T(8,128)}, f32[1024,128]{0,1:T(8,128)}), (f32[1024,128]{0,1:T(8,128)}, f32[1024,128]{0,1:T(8,128)})) %all-reduce.48.cloned.1.call-update) | async-done | bytes 1048592 | tf_op jit(solution)/shard_map/psum | solution.py:42
  954.3 79.8 %all-reduce.68.cloned.1.call-done = (f32[128,128]{0,1:T(8,128)}, f32[128,128]{0,1:T(8,128)}) async-done(((f32[128,128]{0,1:T(8,128)}, f32[128,128]{0,1:T(8,128)}), (f32[128,128]{0,1:T(8,128)}, f32[128,128]{0,1:T(8,128)})) %all-reduce.68.cloned.1.call-update) | async-done | bytes 131088 | tf_op jit(solution)/shard_map/psum | solution.py:43
  1035.9 11.7 cholesky.282
  1048.9 9.8 custom-call.24
  1059.4 3.0 convolution_bitcast_fusion.7
  1062.5 11.7 cholesky.216
  1075.5 10.0 custom-call.18
  1086.1 4.6 convolution_bitcast_fusion.18
  1090.8 88.9 %all-reduce.66.cloned.1.call-done = (f32[1024,128]{0,1:T(8,128)}, f32[1024,128]{0,1:T(8,128)}) async-done(((f32[1024,128]{0,1:T(8,128)}, f32[1024,128]{0,1:T(8,128)}), (f32[1024,128]{0,1:T(8,128)}, f32[1024,128]{0,1:T(8,128)})) %all-reduce.66.cloned.1.call-update) | async-done | bytes 1048592 | tf_op jit(solution)/shard_map/psum | solution.py:30
  1179.7 3.6 convolution_bitcast_fusion.17
  1185.2 122.4 %all-reduce.46.cloned.1.call-done = (f32[1024,128]{0,1:T(8,128)}, f32[1024,128]{0,1:T(8,128)}) async-done(((f32[1024,128]{0,1:T(8,128)}, f32[1024,128]{0,1:T(8,128)}), (f32[1024,128]{0,1:T(8,128)}, f32[1024,128]{0,1:T(8,128)})) %all-reduce.46.cloned.1.call-update) | async-done | bytes 1048592 | tf_op jit(solution)/shard_map/psum | solution.py:42
  1312.8 80.0 %all-reduce.64.cloned.1.call-done = (f32[128,128]{0,1:T(8,128)}, f32[128,128]{0,1:T(8,128)}) async-done(((f32[128,128]{0,1:T(8,128)}, f32[128,128]{0,1:T(8,128)}), (f32[128,128]{0,1:T(8,128)}, f32[128,128]{0,1:T(8,128)})) %all-reduce.64.cloned.1.call-update) | async-done | bytes 131088 | tf_op jit(solution)/shard_map/psum | solution.py:43
  1394.6 11.7 cholesky.293
  1407.6 9.8 custom-call.25
  1418.1 3.0 convolution_bitcast_fusion.5
  1421.2 11.7 cholesky.227
  1434.2 10.2 custom-call.19
  1445.1 4.6 convolution_bitcast_fusion.16
  1449.7 88.9 %all-reduce.62.cloned.1.call-done = (f32[1024,128]{0,1:T(8,128)}, f32[1024,128]{0,1:T(8,128)}) async-done(((f32[1024,128]{0,1:T(8,128)}, f32[1024,128]{0,1:T(8,128)}), (f32[1024,128]{0,1:T(8,128)}, f32[1024,128]{0,1:T(8,128)})) %all-reduce.62.cloned.1.call-update) | async-done | bytes 1048592 | tf_op jit(solution)/shard_map/psum | solution.py:30
  1538.6 3.6 convolution_bitcast_fusion.15
  1544.1 122.4 %all-reduce.44.cloned.1.call-done = (f32[1024,128]{0,1:T(8,128)}, f32[1024,128]{0,1:T(8,128)}) async-done(((f32[1024,128]{0,1:T(8,128)}, f32[1024,128]{0,1:T(8,128)}), (f32[1024,128]{0,1:T(8,128)}, f32[1024,128]{0,1:T(8,128)})) %all-reduce.44.cloned.1.call-update) | async-done | bytes 1048592 | tf_op jit(solution)/shard_map/psum | solution.py:42
  1671.7 80.0 %all-reduce.60.cloned.1.call-done = (f32[128,128]{0,1:T(8,128)}, f32[128,128]{0,1:T(8,128)}) async-done(((f32[128,128]{0,1:T(8,128)}, f32[128,128]{0,1:T(8,128)}), (f32[128,128]{0,1:T(8,128)}, f32[128,128]{0,1:T(8,128)})) %all-reduce.60.cloned.1.call-update) | async-done | bytes 131088 | tf_op jit(solution)/shard_map/psum | solution.py:43
  1753.5 11.7 cholesky.304
  1766.5 9.8 custom-call.26
  1777.0 3.0 convolution_bitcast_fusion.3
  1780.1 11.7 cholesky.238
  1793.1 10.0 custom-call.20
  1803.8 4.6 convolution_bitcast_fusion.14
  1808.4 88.9 %all-reduce.58.cloned.1.call-done = (f32[1024,128]{0,1:T(8,128)}, f32[1024,128]{0,1:T(8,128)}) async-done(((f32[1024,128]{0,1:T(8,128)}, f32[1024,128]{0,1:T(8,128)}), (f32[1024,128]{0,1:T(8,128)}, f32[1024,128]{0,1:T(8,128)})) %all-reduce.58.cloned.1.call-update) | async-done | bytes 1048592 | tf_op jit(solution)/shard_map/psum | solution.py:30
  1897.3 3.6 convolution_bitcast_fusion.13
  1902.9 122.4 %all-reduce.42.cloned.1.call-done = (f32[1024,128]{0,1:T(8,128)}, f32[1024,128]{0,1:T(8,128)}) async-done(((f32[1024,128]{0,1:T(8,128)}, f32[1024,128]{0,1:T(8,128)}), (f32[1024,128]{0,1:T(8,128)}, f32[1024,128]{0,1:T(8,128)})) %all-reduce.42.cloned.1.call-update) | async-done | bytes 1048592 | tf_op jit(solution)/shard_map/psum | solution.py:42
  2030.7 79.8 %all-reduce.56.cloned.1.call-done = (f32[128,128]{0,1:T(8,128)}, f32[128,128]{0,1:T(8,128)}) async-done(((f32[128,128]{0,1:T(8,128)}, f32[128,128]{0,1:T(8,128)}), (f32[128,128]{0,1:T(8,128)}, f32[128,128]{0,1:T(8,128)})) %all-reduce.56.cloned.1.call-update) | async-done | bytes 131088 | tf_op jit(solution)/shard_map/psum | solution.py:43
  2112.2 11.7 cholesky.315
  2125.3 9.8 custom-call.27
  2135.7 3.0 convolution_bitcast_fusion.1
  2138.8 11.7 cholesky.249
  2151.9 10.0 custom-call.21
  2163.3 4.6 convolution_bitcast_fusion
  2168.1 33.5 %psum.316 = f32[32]{0:T(128)S(1)} all-reduce(f32[32]{0:T(128)S(1)} %convert_reduce_fusion), channel_id=1, replica_groups=mesh['dp'=16,'feat'=8] {'dp'}, use_global_device_ids=true, to_apply=%region_39.0 | all-reduce | flops 32 | bytes 256 | tf_op jit(solution)/shard_map/psum | solution.py:50
  2201.7 55.1 %all-reduce.54.cloned.1.call-done = (f32[1024,128]{0,1:T(8,128)}, f32[1024,128]{0,1:T(8,128)}) async-done(((f32[1024,128]{0,1:T(8,128)}, f32[1024,128]{0,1:T(8,128)}), (f32[1024,128]{0,1:T(8,128)}, f32[1024,128]{0,1:T(8,128)})) %all-reduce.54.cloned.1.call-update) | async-done | bytes 1048592 | tf_op jit(solution)/shard_map/psum | solution.py:30
  2261.3 105.7 %all-reduce.40.cloned.1.call-done = f32[128,128]{1,0:T(8,128)} async-done(((f32[128,128]{1,0:T(8,128)}), f32[128,128]{1,0:T(8,128)}) %all-reduce.40.cloned.1.call-update) | async-done | bytes 65552 | tf_op jit(solution)/shard_map/psum | solution.py:54
  (196 shorter events, 88.5 us)
Async XLA Ops:
  7.2 4.5 copy-start
  7.2 4.5 copy-start.17
  7.2 96.4 %all-reduce.78.cloned.1.call-start = ((), (), s32[]{:S(2)}) async-start(), calls=%async_computation.19 | async-start | bytes 2097152 | tf_op jit(solution)/shard_map/psum | solution.py:30
  14.3 216.7 %all-reduce.52.cloned.1.call-start = ((), (), s32[]{:S(2)}) async-start(), calls=%async_computation.6 | async-start | bytes 2097152 | tf_op jit(solution)/shard_map/psum | solution.py:42
  103.6 3.1 copy-start.1
  103.6 3.1 copy-start.18
  108.6 207.5 %all-reduce.76.cloned.1.call-start = ((), (), s32[]{:S(2)}) async-start(), calls=%async_computation.18 | async-start | bytes 262144 | tf_op jit(solution)/shard_map/psum | solution.py:43
  231.0 110.8 %copy-start.9 = (f32[1024,128]{0,1:T(8,128)S(1)}, f32[1024,128]{0,1:T(8,128)}, u32[]{:S(2)}) copy-start(f32[1024,128]{0,1:T(8,128)} %get-tuple-element.22) | copy-start | bytes 1572868
  235.9 227.0 %all-reduce.74.cloned.1.call-start = ((), (), s32[]{:S(2)}) async-start(), calls=%async_computation.17 | async-start | bytes 2097152 | tf_op jit(solution)/shard_map/psum | solution.py:30
  341.8 27.0 %copy-start.3 = (f32[1024,128]{0,1:T(8,128)S(1)}, f32[1024,128]{0,1:T(8,128)}, u32[]{:S(2)}) copy-start(f32[1024,128]{0,1:T(8,128)} %get-tuple-element.21) | copy-start | bytes 1572868
  374.0 216.2 %all-reduce.50.cloned.1.call-start = ((), (), s32[]{:S(2)}) async-start(), calls=%async_computation.5 | async-start | bytes 2097152 | tf_op jit(solution)/shard_map/psum | solution.py:42
  462.9 3.0 copy-start.2
  462.9 3.0 copy-start.19
  467.8 207.6 %all-reduce.72.cloned.1.call-start = ((), (), s32[]{:S(2)}) async-start(), calls=%async_computation.16 | async-start | bytes 262144 | tf_op jit(solution)/shard_map/psum | solution.py:43
  590.2 109.8 %copy-start.10 = (f32[1024,128]{0,1:T(8,128)S(1)}, f32[1024,128]{0,1:T(8,128)}, u32[]{:S(2)}) copy-start(f32[1024,128]{0,1:T(8,128)} %get-tuple-element.20) | copy-start | bytes 1572868
  595.2 225.9 %all-reduce.70.cloned.1.call-start = ((), (), s32[]{:S(2)}) async-start(), calls=%async_computation.15 | async-start | bytes 2097152 | tf_op jit(solution)/shard_map/psum | solution.py:30
  700.0 3.6 copy-start.24
  700.7 26.2 %copy-start.4 = (f32[1024,128]{0,1:T(8,128)S(1)}, f32[1024,128]{0,1:T(8,128)}, u32[]{:S(2)}) copy-start(f32[1024,128]{0,1:T(8,128)} %get-tuple-element.19) | copy-start | bytes 1572868
  732.1 216.9 %all-reduce.48.cloned.1.call-start = ((), (), s32[]{:S(2)}) async-start(), calls=%async_computation.4 | async-start | bytes 2097152 | tf_op jit(solution)/shard_map/psum | solution.py:42
  821.0 3.6 copy-start.20
  826.5 207.6 %all-reduce.68.cloned.1.call-start = ((), (), s32[]{:S(2)}) async-start(), calls=%async_computation.14 | async-start | bytes 262144 | tf_op jit(solution)/shard_map/psum | solution.py:43
  948.9 109.8 %copy-start.11 = (f32[1024,128]{0,1:T(8,128)S(1)}, f32[1024,128]{0,1:T(8,128)}, u32[]{:S(2)}) copy-start(f32[1024,128]{0,1:T(8,128)} %get-tuple-element.18) | copy-start | bytes 1572868
  953.9 225.8 %all-reduce.66.cloned.1.call-start = ((), (), s32[]{:S(2)}) async-start(), calls=%async_computation.13 | async-start | bytes 2097152 | tf_op jit(solution)/shard_map/psum | solution.py:30
  1058.7 3.6 copy-start.25
  1059.4 26.1 %copy-start.5 = (f32[1024,128]{0,1:T(8,128)S(1)}, f32[1024,128]{0,1:T(8,128)}, u32[]{:S(2)}) copy-start(f32[1024,128]{0,1:T(8,128)} %get-tuple-element.17) | copy-start | bytes 1572868
  1090.7 216.9 %all-reduce.46.cloned.1.call-start = ((), (), s32[]{:S(2)}) async-start(), calls=%async_computation.3 | async-start | bytes 2097152 | tf_op jit(solution)/shard_map/psum | solution.py:42
  1179.7 3.6 copy-start.21
  1185.2 207.6 %all-reduce.64.cloned.1.call-start = ((), (), s32[]{:S(2)}) async-start(), calls=%async_computation.12 | async-start | bytes 262144 | tf_op jit(solution)/shard_map/psum | solution.py:43
  1307.7 109.8 %copy-start.12 = (f32[1024,128]{0,1:T(8,128)S(1)}, f32[1024,128]{0,1:T(8,128)}, u32[]{:S(2)}) copy-start(f32[1024,128]{0,1:T(8,128)} %get-tuple-element.16) | copy-start | bytes 1572868
  1312.6 226.0 %all-reduce.62.cloned.1.call-start = ((), (), s32[]{:S(2)}) async-start(), calls=%async_computation.11 | async-start | bytes 2097152 | tf_op jit(solution)/shard_map/psum | solution.py:30
  1417.5 3.6 copy-start.26
  1418.1 26.3 %copy-start.6 = (f32[1024,128]{0,1:T(8,128)S(1)}, f32[1024,128]{0,1:T(8,128)}, u32[]{:S(2)}) copy-start(f32[1024,128]{0,1:T(8,128)} %get-tuple-element.15) | copy-start | bytes 1572868
  1449.7 216.9 %all-reduce.44.cloned.1.call-start = ((), (), s32[]{:S(2)}) async-start(), calls=%async_computation.2 | async-start | bytes 2097152 | tf_op jit(solution)/shard_map/psum | solution.py:42
  1538.6 3.6 copy-start.22
  1544.1 207.6 %all-reduce.60.cloned.1.call-start = ((), (), s32[]{:S(2)}) async-start(), calls=%async_computation.10 | async-start | bytes 262144 | tf_op jit(solution)/shard_map/psum | solution.py:43
  1666.5 109.8 %copy-start.13 = (f32[1024,128]{0,1:T(8,128)S(1)}, f32[1024,128]{0,1:T(8,128)}, u32[]{:S(2)}) copy-start(f32[1024,128]{0,1:T(8,128)} %get-tuple-element.14) | copy-start | bytes 1572868
  1671.5 225.9 %all-reduce.58.cloned.1.call-start = ((), (), s32[]{:S(2)}) async-start(), calls=%async_computation.9 | async-start | bytes 2097152 | tf_op jit(solution)/shard_map/psum | solution.py:30
  1776.3 3.6 copy-start.27
  1777.0 26.2 %copy-start.7 = (f32[1024,128]{0,1:T(8,128)S(1)}, f32[1024,128]{0,1:T(8,128)}, u32[]{:S(2)}) copy-start(f32[1024,128]{0,1:T(8,128)} %get-tuple-element.13) | copy-start | bytes 1572868
  1808.4 216.9 %all-reduce.42.cloned.1.call-start = ((), (), s32[]{:S(2)}) async-start(), calls=%async_computation.1 | async-start | bytes 2097152 | tf_op jit(solution)/shard_map/psum | solution.py:42
  1897.3 3.6 copy-start.23
  1902.8 207.6 %all-reduce.56.cloned.1.call-start = ((), (), s32[]{:S(2)}) async-start(), calls=%async_computation.8 | async-start | bytes 262144 | tf_op jit(solution)/shard_map/psum | solution.py:43
  2025.3 109.8 %copy-start.14 = (f32[1024,128]{0,1:T(8,128)S(1)}, f32[1024,128]{0,1:T(8,128)}, u32[]{:S(2)}) copy-start(f32[1024,128]{0,1:T(8,128)} %get-tuple-element.12) | copy-start | bytes 1572868
  2030.2 226.6 %all-reduce.54.cloned.1.call-start = ((), (), s32[]{:S(2)}) async-start(), calls=%async_computation.7 | async-start | bytes 2097152 | tf_op jit(solution)/shard_map/psum | solution.py:30
  2135.1 3.6 copy-start.28
  2135.7 26.1 %copy-start.8 = (f32[1024,128]{0,1:T(8,128)S(1)}, f32[1024,128]{0,1:T(8,128)}, u32[]{:S(2)}) copy-start(f32[1024,128]{0,1:T(8,128)} %get-tuple-element.11) | copy-start | bytes 1572868
  2162.5 0.8 copy-start.15
  2163.3 4.7 copy-start.29
  2167.9 92.4 %copy-start.16 = (f32[128,1024]{1,0:T(8,128)S(1)}, f32[128,1024]{1,0:T(8,128)}, u32[]{:S(2)}) copy-start(f32[128,1024]{1,0:T(8,128)} %copy-done.15) | copy-start | bytes 1572868
  2167.9 199.1 %all-reduce.40.cloned.1.call-start = ((), (), s32[]{:S(2)}) async-start(), calls=%async_computation | async-start | bytes 131072 | tf_op jit(solution)/shard_map/psum | solution.py:54
Sparse Core Ops, SparseCore 0:
  14.4 89.1 all-reduce.77
  108.8 122.1 all-reduce.51
  236.0 80.0 all-reduce.75
  374.1 88.7 all-reduce.73
  467.9 122.2 all-reduce.49
  595.3 80.0 all-reduce.71
  732.2 88.7 all-reduce.69
  826.6 122.2 all-reduce.47
  954.0 80.0 all-reduce.67
  1090.9 88.7 all-reduce.65
  1185.3 122.3 all-reduce.45
  1312.7 80.0 all-reduce.63
  1449.8 88.7 all-reduce.61
  1544.2 122.2 all-reduce.43
  1671.6 80.0 all-reduce.59
  1808.5 88.7 all-reduce.57
  1902.9 122.3 all-reduce.41
  2030.3 80.0 all-reduce.55
  2168.0 88.7 all-reduce.53
  2259.7 107.2 all-reduce.39
where the time goes:
time: 2380 us
  waiting for transfers between devices  1910 us (80%)
  other arithmetic  281 us (12%)
  matrix products  123 us (5%)
  blocking collectives  33.5 us (1%)
    psum x6, waiting for transfers between devices, local(): summed = lax.psum((images[0], images[1]), 'dp')  734 us
    psum x7, waiting for transfers between devices, project(): lax.psum((jnp.dot(act_wide, basis[0], precision=highest), jnp.dot(grad_wi...  589 us
    psum x6, waiting for transfers between devices, local(): grams = lax.psum((gram_of(summed[0]), gram_of(summed[1])), 'feat')  479 us
    another operation x36, other arithmetic, orthonormal(): lower = jnp.linalg.cholesky(gram_mat)  149 us
    another operation x24, other arithmetic, orthonormal(): return jax.scipy.linalg.solve_triangular(lower, image.T, lower=True).T  127 us
    psum x1, waiting for transfers between devices, local(): scales = lax.psum(partial_scales, 'dp')  106 us
  transfers between devices with their start and end apart: 20, of which 20 were waited for; matrix products, arithmetic and copies ran while one was open for 0% of the time, Pallas kernels for 0%

commit v1 on v0

v1 whole, which is shorter than its diff:
```python
import functools

import jax
import jax.numpy as jnp
from jax import lax
from jax.experimental import pallas as pl
from jax.experimental.pallas import tpu as pltpu
from jax.sharding import PartitionSpec as P

ITERS = 6
K = 128
MESH = pl.DeviceIdType.MESH
F32 = jnp.float32
BF16 = jnp.bfloat16
HIGHEST = lax.Precision.HIGHEST

OFFSETS = ((2, 1), (1, 1), (3, 1), (2, 0), (0, 1), (1, 0), (3, 0))


def pieces(value):
    high = value.astype(BF16)
    rest = value - high.astype(F32)
    mid = rest.astype(BF16)
    low = (rest - mid.astype(F32)).astype(BF16)
    return jnp.concatenate([high, mid, low], axis=1)


def joined(product):
    return product[:, :K] + (product[:, K : 2 * K] + product[:, 2 * K :])


def times(a, b):
    return lax.dot_general(a, b, (((1,), (0,)), ((), ())), preferred_element_type=F32)


def full(a, b, contract):
    return lax.dot_general(
        a, b, ((contract[:1], contract[1:]), ((), ())), precision=HIGHEST, preferred_element_type=F32
    )


def kernel(
    act_ref, grad_ref, start_act_ref, start_grad_ref, ids_ref,
    basis_act_ref, basis_grad_ref, scales_ref,
    x_send, x_recv, x, xt, split,
    y_send, y_recv, p, v_send, v_recv, v,
    g_send, g_recv, g, work, inverse,
    ids, c_recv, proj_mine, proj_other, basis_mine, basis_other,
    s_part, s_feat, s_dp, s_mine, s_other,
    x_sems, y_ssem, y_rsem, p_ssem, p_rsem, v_ssem, v_rsem, w_ssem, w_rsem,
    gs_ssem, gs_rsem, ga_ssem, ga_rsem, c_ssem, c_rsem, core_ssem, core_rsem,
    sf_ssem, sf_rsem, sd_ssem, sd_rsem,
):
    dp, feat = lax.axis_index("dp"), lax.axis_index("feat")
    core, q = dp % 2, dp // 2
    px, py = q % 4, q // 4
    fz, fy = feat // 2, feat % 2

    def feat_peer(r):
        dz, dy = OFFSETS[r]
        return ((fz + dz) % 4) * 2 + (fy + dy) % 2

    def feat_from(r):
        dz, dy = OFFSETS[r]
        return ((fz + 4 - dz) % 4) * 2 + (fy + dy) % 2

    def q_peer(r):
        dx, dy = OFFSETS[r]
        return ((py + dy) % 2) * 4 + (px + dx) % 4

    def q_from(r):
        dx, dy = OFFSETS[r]
        return ((py + dy) % 2) * 4 + (px + 4 - dx) % 4

    def to_feat(r, src, dst, ssem, rsem):
        return pltpu.make_async_remote_copy(
            src_ref=src, dst_ref=dst, send_sem=ssem.at[r], recv_sem=rsem.at[r],
            device_id={"feat": feat_peer(r)}, device_id_type=MESH,
        )

    def to_dp(r, src, dst, ssem, rsem):
        return pltpu.make_async_remote_copy(
            src_ref=src, dst_ref=dst, send_sem=ssem.at[r], recv_sem=rsem.at[r],
            device_id={"dp": q_peer(r) * 2 + core}, device_id_type=MESH,
        )

    def to_core(i, src, dst):
        return pltpu.make_async_remote_copy(
            src_ref=src, dst_ref=dst, send_sem=core_ssem.at[i], recv_sem=core_rsem.at[i],
            device_id={"dp": q * 2 + (1 - core)}, device_id_type=MESH,
        )

    barrier = pltpu.get_barrier_semaphore()
    for r in range(7):
        pl.semaphore_signal(barrier, inc=1, device_id={"feat": feat_peer(r)}, device_id_type=MESH)
        pl.semaphore_signal(
            barrier, inc=1, device_id={"dp": q_peer(r) * 2 + core}, device_id_type=MESH
        )
    pl.semaphore_signal(
        barrier, inc=1, device_id={"dp": q * 2 + (1 - core)}, device_id_type=MESH
    )
    pl.semaphore_wait(barrier, 15)

    even = core == 0
    ids_own = pl.ds(pl.multiple_of(core * 8, 8), 8)
    ids[ids_own, :] = ids_ref[...]
    ids_copy = to_core(0, ids.at[ids_own, :], ids.at[ids_own, :])
    ids_copy.start()
    x_copies = []
    for i in range(4):
        rows = slice(i * 256, (i + 1) * 256)
        x_send[rows, :] = jnp.where(even, grad_ref[rows, :].astype(F32), act_ref[rows, :].astype(F32))
        copy = pltpu.make_async_remote_copy(
            src_ref=x_send.at[rows, :], dst_ref=x_recv.at[rows, :],
            send_sem=x_sems.at[0, i], recv_sem=x_sems.at[1, i],
            device_id={"dp": q * 2 + (1 - core)}, device_id_type=MESH,
        )
        copy.start()
        x_copies.append(copy)
    for i in range(4):
        rows = slice(i * 256, (i + 1) * 256)
        x[pl.ds(pl.multiple_of(core * 1024 + i * 256, 256), 256), :] = jnp.where(
            even, act_ref[rows, :].astype(F32), grad_ref[rows, :].astype(F32)
        ).astype(BF16)
    v[...] = jnp.where(even, start_act_ref[...], start_grad_ref[...])
    lane = lax.broadcasted_iota(jnp.int32, (K, K), 1)
    row = lax.broadcasted_iota(jnp.int32, (K, K), 0)
    inverse[...] = (lane == row).astype(F32)
    for i in range(4):
        x_copies[i].wait()
        x[pl.ds(pl.multiple_of((1 - core) * 1024 + i * 256, 256), 256), :] = x_recv[
            i * 256 : (i + 1) * 256, :
        ].astype(BF16)

    def token_rows(f):
        return pl.ds(pl.multiple_of(f * 256, 256), 256)

    def feature_rows(i):
        return pl.ds(pl.multiple_of(i * 128, 128), 128)

    def gram_rows(f):
        return pl.ds(pl.multiple_of(f * 16, 16), 16)

    def project():
        split[...] = pieces(v[...])
        copies = []
        for r in range(7):
            rows = token_rows(feat_peer(r))
            y_send[rows, :] = joined(times(x[rows, :], split[...]))
            copy = to_feat(r, y_send.at[rows, :], y_recv.at[r], y_ssem, y_rsem)
            copy.start()
            copies.append(copy)
        rows = token_rows(feat)
        y_send[rows, :] = joined(times(x[rows, :], split[...]))
        return copies

    def projected(copies):
        for copy in copies:
            copy.wait()
        total = y_send[token_rows(feat), :]
        for r in range(7):
            total = total + y_recv[r]
        return total

    def gram_send():
        image = v[...]
        g_send[...] = full(image, image, (0, 0))
        copies = []
        for r in range(7):
            copy = to_feat(r, g_send.at[gram_rows(feat_peer(r)), :], g_recv.at[r], gs_ssem, gs_rsem)
            copy.start()
            copies.append(copy)
        return copies

    def gram_copies():
        return [
            to_feat(r, g_send.at[gram_rows(feat_peer(r)), :], g_recv.at[r], gs_ssem, gs_rsem)
            for r in range(7)
        ]

    def gram_gathers():
        mine = gram_rows(feat)
        return [to_feat(r, g.at[mine, :], g.at[mine, :], ga_ssem, ga_rsem) for r in range(7)]

    def gram_sum():
        for copy in gram_copies():
            copy.wait()
        total = g_send[gram_rows(feat), :]
        for r in range(7):
            total = total + g_recv[r]
        g[gram_rows(feat), :] = total
        for copy in gram_gathers():
            copy.start()

    def factor():
        for copy in gram_gathers():
            copy.wait()
        work[:, :K] = g[...]
        work[:, K:] = (lane == row).astype(F32)
        small_row = lax.broadcasted_iota(jnp.int32, (8, K), 0)
        small_lane = lax.broadcasted_iota(jnp.int32, (8, K), 1)
        wide_row = lax.broadcasted_iota(jnp.int32, (K, 2 * K), 0)

        def panel(i, _):
            at = pl.ds(pl.multiple_of(i * 8, 8), 8)
            strip = work[at, :]
            block = pltpu.roll(strip[:, :K], (K - i * 8) % K, 1)
            block = jnp.where(small_lane < 8, block, (small_lane - 8 == small_row).astype(F32))
            for j in range(8):
                column = block[:, j : j + 1]
                pivot = block[j : j + 1, j : j + 1]
                scale = lax.rsqrt(pivot)
                scale = scale * (1.5 - 0.5 * pivot * scale * scale)
                normal = block[j : j + 1, :] * scale
                below = block - (column * scale) * normal
                block = jnp.where(small_row > j, below, jnp.where(small_row == j, normal, block))
            fresh = jnp.zeros_like(strip)
            for j in range(8):
                fresh = fresh + block[:, 8 + j : 9 + j] * strip[j : j + 1, :]
            update = full(fresh[:, :K], fresh, (0, 0))
            work[...] = jnp.where(wide_row >= i * 8 + 8, work[...] - update, work[...])
            work[at, :] = fresh
            return 0

        lax.fori_loop(0, 16, panel, 0)
        inverse[...] = work[:, K:]

    def sweep(step, _):
        y_copies = project()

        @pl.when(step > 0)
        def _():
            gram_send()

        @pl.when(step == 0)
        def _():
            for c in range(8):
                xt[c] = x[c * 256 : (c + 1) * 256, :].T

        total = projected(y_copies)
        mine = token_rows(feat)
        p[mine, :] = total
        p_copies = [to_feat(r, p.at[mine, :], p.at[mine, :], p_ssem, p_rsem) for r in range(7)]

        @pl.when(step > 0)
        def _():
            gram_sum()

        for copy in p_copies:
            copy.start()
        v_send[...] = joined(times(xt[feat], pieces(p[mine, :])))

        @pl.when(step > 0)
        def _():
            factor()

        for r in reversed(range(7)):
            p_copies[r].wait()
            source = feat_from(r)
            v_send[...] += joined(times(xt[source], pieces(p[token_rows(source), :])))

        own = feature_rows(q)
        v_copies = []
        for r in range(7):
            copy = to_dp(r, v_send.at[feature_rows(q_peer(r)), :], v_recv.at[r], v_ssem, v_rsem)
            copy.start()
            v_copies.append(copy)
        for copy in v_copies:
            copy.wait()
        total = v_send[own, :]
        for r in range(7):
            total = total + v_recv[r]
        v[own, :] = full(total, inverse[...], (1, 1))
        w_copies = [to_dp(r, v.at[own, :], v.at[own, :], w_ssem, w_rsem) for r in range(7)]
        for copy in w_copies:
            copy.start()
        for copy in w_copies:
            copy.wait()
        return 0

    lax.fori_loop(0, ITERS, sweep, 0)

    y_copies = project()
    gram_send()
    ids_copy.wait()
    counts = jnp.zeros((1, K), F32)
    for i in range(16):
        column = jnp.broadcast_to(ids[i : i + 1, :].astype(F32), (K, K)).T
        counts = counts + jnp.sum((column == lane.astype(F32)).astype(F32), axis=0, keepdims=True)
    c_recv[q] = jnp.broadcast_to(counts, (8, K))
    c_copies = [to_dp(r, c_recv.at[q], c_recv.at[q], c_ssem, c_rsem) for r in range(7)]
    for copy in c_copies:
        copy.start()

    total = projected(y_copies)
    gram_sum()
    factor()
    basis_mine[...] = full(v[...], inverse[...], (1, 1))
    proj_mine[...] = full(total, inverse[...], (1, 1))
    proj_copy = to_core(1, proj_mine, proj_other)
    proj_copy.start()
    basis_copy = to_core(2, basis_mine, basis_other)
    basis_copy.start()
    for copy in c_copies:
        copy.wait()
    counts = c_recv[0]
    for i in range(1, 8):
        counts = counts + c_recv[i]
    counts = counts[0:1, :]
    documents = 2 * lax.axis_size("dp")
    share = jnp.where(counts > 0, 1.0 / (documents * jnp.maximum(counts, 1.0)), 0.0)
    weight = []
    for i in range(2):
        column = jnp.broadcast_to(ids[pl.ds(feat * 2 + i, 1), :].astype(F32), (K, K)).T
        weight.append(
            jnp.sum(jnp.where(column == lane.astype(F32), share, 0.0), axis=1, keepdims=True)
        )
    proj_copy.wait()
    proj_act = jnp.where(even, proj_mine[...], proj_other[...])
    proj_grad = jnp.where(even, proj_other[...], proj_mine[...])
    left = jnp.concatenate(weight, axis=0) * proj_grad * proj_grad
    s_part[...] = full(left, proj_act * proj_act, (0, 0))

    half = pl.ds(pl.multiple_of(core * 64, 64), 64)
    s_feat[feat] = s_part[half, :]
    copies = [to_feat(r, s_feat.at[feat], s_feat.at[feat], sf_ssem, sf_rsem) for r in range(7)]
    for copy in copies:
        copy.start()
    for copy in copies:
        copy.wait()
    total = s_feat[0]
    for i in range(1, 8):
        total = total + s_feat[i]
    s_dp[q] = total
    copies = [to_dp(r, s_dp.at[q], s_dp.at[q], sd_ssem, sd_rsem) for r in range(7)]
    for copy in copies:
        copy.start()
    basis_copy.wait()
    basis_act_ref[...] = jnp.where(even, basis_mine[...], basis_other[...])
    basis_grad_ref[...] = jnp.where(even, basis_other[...], basis_mine[...])
    for copy in copies:
        copy.wait()
    total = s_dp[0]
    for i in range(1, 8):
        total = total + s_dp[i]
    s_mine[...] = total
    s_copy = to_core(3, s_mine, s_other)
    s_copy.start()
    s_copy.wait()
    scales_ref[half, :] = s_mine[...]
    scales_ref[pl.ds(pl.multiple_of((1 - core) * 64, 64), 64), :] = s_other[...]


def local(activations, gradients, start_act, start_grad, doc_ids):
    vmem = pl.BlockSpec(memory_space=pltpu.VMEM)
    dma = pltpu.SemaphoreType.DMA
    return pl.pallas_call(
        kernel,
        out_shape=(
            jax.ShapeDtypeStruct((1024, K), F32),
            jax.ShapeDtypeStruct((1024, K), F32),
            jax.ShapeDtypeStruct((K, K), F32),
        ),
        in_specs=[vmem] * 5,
        out_specs=(vmem,) * 3,
        scratch_shapes=[
            pltpu.VMEM((1024, 1024), F32),
            pltpu.VMEM((1024, 1024), F32),
            pltpu.VMEM((2048, 1024), BF16),
            pltpu.VMEM((8, 1024, 256), BF16),
            pltpu.VMEM((1024, 3 * K), BF16),
            pltpu.VMEM((2048, K), F32),
            pltpu.VMEM((7, 256, K), F32),
            pltpu.VMEM((2048, K), F32),
            pltpu.VMEM((1024, K), F32),
            pltpu.VMEM((7, 128, K), F32),
            pltpu.VMEM((1024, K), F32),
            pltpu.VMEM((K, K), F32),
            pltpu.VMEM((7, 16, K), F32),
            pltpu.VMEM((K, K), F32),
            pltpu.VMEM((K, 2 * K), F32),
            pltpu.VMEM((K, K), F32),
            pltpu.VMEM((16, K), jnp.int32),
            pltpu.VMEM((8, 8, K), F32),
            pltpu.VMEM((256, K), F32),
            pltpu.VMEM((256, K), F32),
            pltpu.VMEM((1024, K), F32),
            pltpu.VMEM((1024, K), F32),
            pltpu.VMEM((K, K), F32),
            pltpu.VMEM((8, 64, K), F32),
            pltpu.VMEM((8, 64, K), F32),
            pltpu.VMEM((64, K), F32),
            pltpu.VMEM((64, K), F32),
            dma((2, 4)),
            dma((7,)), dma((7,)), dma((7,)), dma((7,)), dma((7,)), dma((7,)), dma((7,)), dma((7,)),
            dma((7,)), dma((7,)), dma((7,)), dma((7,)), dma((7,)), dma((7,)), dma((4,)), dma((4,)),
            dma((7,)), dma((7,)), dma((7,)), dma((7,)),
        ],
        compiler_params=pltpu.CompilerParams(
            collective_id=0, has_side_effects=True, vmem_limit_bytes=48 * 2**20
        ),
        name="subspace",
    )(activations, gradients, start_act, start_grad, doc_ids.reshape(8, 128))


def solution(mesh):
    placed = (P("dp", "feat"), P("dp", "feat"), P("feat", None), P("feat", None), P("dp"))
    return jax.shard_map(
        local,
        mesh=mesh,
        in_specs=placed,
        out_specs=(P("feat", None), P("feat", None), P()),
        check_vma=False,
    )
```

time: 2380 us -> 404 us (0.17)
  waiting for transfers between devices: 1910 us -> 0 us
  Pallas kernels: 0 us -> 396 us
  other arithmetic: 281 us -> 0 us
  matrix products: 123 us -> 0 us
  blocking collectives: 33.5 us -> 0 us
    psum x20 -> x0, waiting for transfers between devices: 1910 us -> none  [the longest x6 734 us: local(): summed = lax.psum((images[0], images[1]), 'dp')]
    pallas_call x0 -> x1, Pallas kernels: none -> 396 us  [local(): pl.pallas_call(kernel, out_shape=(jax.ShapeDtypeStruct((1024, K), F32), j...]
    another operation x60 -> x0, other arithmetic: 276 us -> none  [the longest x36 149 us: orthonormal(): lower = jnp.linalg.cholesky(gram_mat)]
    dot_general x40 -> x0, matrix products: 116 us -> none  [the longest x13 34 us: tokens_contract(): lax.dot_general(wide, projected, (((0,), (0,)), ((), ())), precision=high...]
    psum x1 -> x0, blocking collectives: 33.5 us -> none  [local(): counts = lax.psum(jnp.sum(onehot, axis=0), 'dp')]
  transfers between devices with their start and end apart: 20 -> 0, of which waited for: 20 -> 0; matrix products, arithmetic and copies ran while one was open for 0% -> 0% of each run, Pallas kernels for 0% -> 0%
where the time goes in v1:
time: 404 us; the launch traced here: 403 us
  Pallas kernels  396 us (98%)
  local copies, waits for them, and re-layouts  6.57 us (2%)
    pallas_call x1, Pallas kernels, local(): pl.pallas_call(kernel, out_shape=(jax.ShapeDtypeStruct((1024, K), F32), j...  396 us

profile of v1, /device:TPU:1, one launch (start us, length us, event | category | flops | bytes accessed | tf_op | source)
XLA Modules:
  0.0 403.3 jit_solution(9244596619611284664)
XLA Ops:
  0.6 0.0 copy-start
  0.6 1.6 copy-done
  2.2 0.0 copy-start.1
  2.2 1.0 copy-done.1
  3.3 0.0 copy-start.2
  3.3 1.0 copy-done.2
  4.3 0.0 copy-start.3
  4.3 0.7 copy-done.3
  5.0 396.1 %subspace.1 = (f32[1024,128]{1,0:T(8,128)S(1)}, f32[1024,128]{1,0:T(8,128)S(1)}, f32[128,128]{1,0:T(8,128)S(1)}) custom-call(bf16[1024,1024]{1,0:T(8,128)(2,1)S(1)} %copy-done, bf16[1024,1024]{1,0:T(8,128)(2,1)} %grad_ref.1, f32[1024,128]{1,0:T(8,128)S(1)} %copy-done.1, f32[1024,128]{1,0:T(8,128)S(1)} %copy-done.2, s32[8,128]{1,0:T(8,128)S(1)} %bitcast.1), custom_call_target="tpu_custom_call" | custom-call | tf_op jit(solution)/shard_map/subspace/pallas_call | solution.py:357
  401.1 0.8 copy.11
  401.9 0.8 copy.12
  402.7 0.6 copy.13
Async XLA Ops:
  0.6 1.6 copy-start
  2.2 1.0 copy-start.1
  3.3 1.0 copy-start.2
  4.3 0.7 copy-start.3

commit v2 on v1

--- a/solution.py
+++ b/solution.py
@@ -135,31 +135,34 @@
     def token_rows(f):
         return pl.ds(pl.multiple_of(f * 256, 256), 256)
 
-    def feature_rows(i):
-        return pl.ds(pl.multiple_of(i * 128, 128), 128)
-
     def gram_rows(f):
         return pl.ds(pl.multiple_of(f * 16, 16), 16)
 
+    def half_rows(f, h):
+        return pl.ds(pl.multiple_of(f * 256 + h * 128, 128), 128)
+
+    def y_copy(r, h):
+        return to_feat(
+            r, y_send.at[half_rows(feat_peer(r), h), :], y_recv.at[r, h], y_ssem.at[h], y_rsem.at[h]
+        )
+
     def project():
         split[...] = pieces(v[...])
-        copies = []
         for r in range(7):
             rows = token_rows(feat_peer(r))
             y_send[rows, :] = joined(times(x[rows, :], split[...]))
-            copy = to_feat(r, y_send.at[rows, :], y_recv.at[r], y_ssem, y_rsem)
-            copy.start()
-            copies.append(copy)
+            y_copy(r, 0).start()
+        for r in range(7):
+            y_copy(r, 1).start()
         rows = token_rows(feat)
         y_send[rows, :] = joined(times(x[rows, :], split[...]))
-        return copies
-
-    def projected(copies):
-        for copy in copies:
-            copy.wait()
-        total = y_send[token_rows(feat), :]
-        for r in range(7):
-            total = total + y_recv[r]
+
+    def projected(h):
+        for r in range(7):
+            y_copy(r, h).wait()
+        total = y_send[half_rows(feat, h), :]
+        for r in range(7):
+            total = total + y_recv[r, h]
         return total
 
     def gram_send():
@@ -192,41 +195,62 @@
         for copy in gram_gathers():
             copy.start()
 
-    def factor():
+    def eliminate(first, last):
+        small_row = lax.broadcasted_iota(jnp.int32, (8, K), 0)
+        wide_row = lax.broadcasted_iota(jnp.int32, (K, 2 * K), 0)
+
+        def panel(i, _):
+            at = pl.ds(pl.multiple_of(i * 8, 8), 8)
+            left, right = work[at, :K], work[at, K:]
+            block = pltpu.roll(left, (K - i * 8) % K, 1)
+            column = [jnp.broadcast_to(block[:, j : j + 1], (8, K)) for j in range(8)]
+            pivots = jnp.ones((8, K), F32)
+            for j in range(8):
+                pivot = jnp.broadcast_to(column[j][j : j + 1, :], (8, K))
+                ratio = jnp.where(small_row > j, column[j] * (1.0 / pivot), 0.0)
+                pivots = jnp.where(small_row == j, pivot, pivots)
+                for k in range(j + 1, 8):
+                    column[k] = column[k] - ratio * column[k][j : j + 1, :]
+                left = left - ratio * left[j : j + 1, :]
+                right = right - ratio * right[j : j + 1, :]
+            scale = lax.rsqrt(pivots)
+            scale = scale * (1.5 - 0.5 * pivots * scale * scale)
+            fresh = jnp.concatenate([left * scale, right * scale], axis=1)
+            update = full(fresh[:, :K], fresh, (0, 0))
+            work[...] = jnp.where(wide_row >= i * 8 + 8, work[...] - update, work[...])
+            work[at, :] = fresh
+            return 0
+
+        lax.fori_loop(first, last, panel, 0)
+
+    def factor_start():
         for copy in gram_gathers():
             copy.wait()
         work[:, :K] = g[...]
         work[:, K:] = (lane == row).astype(F32)
-        small_row = lax.broadcasted_iota(jnp.int32, (8, K), 0)
-        small_lane = lax.broadcasted_iota(jnp.int32, (8, K), 1)
-        wide_row = lax.broadcasted_iota(jnp.int32, (K, 2 * K), 0)
-
-        def panel(i, _):
-            at = pl.ds(pl.multiple_of(i * 8, 8), 8)
-            strip = work[at, :]
-            block = pltpu.roll(strip[:, :K], (K - i * 8) % K, 1)
-            block = jnp.where(small_lane < 8, block, (small_lane - 8 == small_row).astype(F32))
-            for j in range(8):
-                column = block[:, j : j + 1]
-                pivot = block[j : j + 1, j : j + 1]
-                scale = lax.rsqrt(pivot)
-                scale = scale * (1.5 - 0.5 * pivot * scale * scale)
-                normal = block[j : j + 1, :] * scale
-                below = block - (column * scale) * normal
-                block = jnp.where(small_row > j, below, jnp.where(small_row == j, normal, block))
-            fresh = jnp.zeros_like(strip)
-            for j in range(8):
-                fresh = fresh + block[:, 8 + j : 9 + j] * strip[j : j + 1, :]
-            update = full(fresh[:, :K], fresh, (0, 0))
-            work[...] = jnp.where(wide_row >= i * 8 + 8, work[...] - update, work[...])
-            work[at, :] = fresh
-            return 0
-
-        lax.fori_loop(0, 16, panel, 0)
+        eliminate(0, 8)
+
+    def factor_end():
+        eliminate(8, 16)
         inverse[...] = work[:, K:]
 
+    def p_copy(r, h):
+        mine = half_rows(feat, h)
+        return to_feat(r, p.at[mine, :], p.at[mine, :], p_ssem.at[h], p_rsem.at[h])
+
+    def v_copy(r, h):
+        rows = part_rows(q_peer(r), h)
+        return to_dp(r, v_send.at[rows, :], v_recv.at[r, h], v_ssem.at[h], v_rsem.at[h])
+
+    def w_copy(r, h):
+        mine = part_rows(q, h)
+        return to_dp(r, v.at[mine, :], v.at[mine, :], w_ssem.at[h], w_rsem.at[h])
+
+    def part_rows(i, h):
+        return pl.ds(pl.multiple_of(i * 128 + h * 64, 64), 64)
+
     def sweep(step, _):
-        y_copies = project()
+        project()
 
         @pl.when(step > 0)
         def _():
@@ -234,53 +258,63 @@
 
         @pl.when(step == 0)
         def _():
-            for c in range(8):
-                xt[c] = x[c * 256 : (c + 1) * 256, :].T
-
-        total = projected(y_copies)
-        mine = token_rows(feat)
-        p[mine, :] = total
-        p_copies = [to_feat(r, p.at[mine, :], p.at[mine, :], p_ssem, p_rsem) for r in range(7)]
+            for c in range(16):
+                xt[c] = x[c * 128 : (c + 1) * 128, :].T
+
+        p[half_rows(feat, 0), :] = projected(0)
 
         @pl.when(step > 0)
         def _():
             gram_sum()
 
-        for copy in p_copies:
-            copy.start()
-        v_send[...] = joined(times(xt[feat], pieces(p[mine, :])))
+        for r in range(7):
+            p_copy(r, 0).start()
+        p[half_rows(feat, 1), :] = projected(1)
+        for r in range(7):
+            p_copy(r, 1).start()
 
         @pl.when(step > 0)
         def _():
-            factor()
-
-        for r in reversed(range(7)):
-            p_copies[r].wait()
-            source = feat_from(r)
-            v_send[...] += joined(times(xt[source], pieces(p[token_rows(source), :])))
-
-        own = feature_rows(q)
-        v_copies = []
-        for r in range(7):
-            copy = to_dp(r, v_send.at[feature_rows(q_peer(r)), :], v_recv.at[r], v_ssem, v_rsem)
-            copy.start()
-            v_copies.append(copy)
-        for copy in v_copies:
-            copy.wait()
-        total = v_send[own, :]
-        for r in range(7):
-            total = total + v_recv[r]
-        v[own, :] = full(total, inverse[...], (1, 1))
-        w_copies = [to_dp(r, v.at[own, :], v.at[own, :], w_ssem, w_rsem) for r in range(7)]
-        for copy in w_copies:
-            copy.start()
-        for copy in w_copies:
-            copy.wait()
+            factor_start()
+
+        for h in range(2):
+            part = joined(times(xt[feat * 2 + h], pieces(p[half_rows(feat, h), :])))
+            if h == 0:
+                v_send[...] = part
+            else:
+                v_send[...] += part
+            for r in reversed(range(7)):
+                p_copy(r, h).wait()
+                source = feat_from(r)
+                v_send[...] += joined(
+                    times(xt[source * 2 + h], pieces(p[half_rows(source, h), :]))
+                )
+
+        for h in range(2):
+            for r in range(7):
+                v_copy(r, h).start()
+
+        @pl.when(step > 0)
+        def _():
+            factor_end()
+
+        for h in range(2):
+            for r in range(7):
+                v_copy(r, h).wait()
+            total = v_send[part_rows(q, h), :]
+            for r in range(7):
+                total = total + v_recv[r, h]
+            v[part_rows(q, h), :] = full(total, inverse[...], (1, 1))
+            for r in range(7):
+                w_copy(r, h).start()
+        for h in range(2):
+            for r in range(7):
+                w_copy(r, h).wait()
         return 0
 
     lax.fori_loop(0, ITERS, sweep, 0)
 
-    y_copies = project()
+    project()
     gram_send()
     ids_copy.wait()
     counts = jnp.zeros((1, K), F32)
@@ -292,9 +326,10 @@
     for copy in c_copies:
         copy.start()
 
-    total = projected(y_copies)
     gram_sum()
-    factor()
+    total = jnp.concatenate([projected(0), projected(1)], axis=0)
+    factor_start()
+    factor_end()
     basis_mine[...] = full(v[...], inverse[...], (1, 1))
     proj_mine[...] = full(total, inverse[...], (1, 1))
     proj_copy = to_core(1, proj_mine, proj_other)
@@ -367,13 +402,13 @@
             pltpu.VMEM((1024, 1024), F32),
             pltpu.VMEM((1024, 1024), F32),
             pltpu.VMEM((2048, 1024), BF16),
-            pltpu.VMEM((8, 1024, 256), BF16),
+            pltpu.VMEM((16, 1024, 128), BF16),
             pltpu.VMEM((1024, 3 * K), BF16),
             pltpu.VMEM((2048, K), F32),
-            pltpu.VMEM((7, 256, K), F32),
+            pltpu.VMEM((7, 2, 128, K), F32),
             pltpu.VMEM((2048, K), F32),
             pltpu.VMEM((1024, K), F32),
-            pltpu.VMEM((7, 128, K), F32),
+            pltpu.VMEM((7, 2, 64, K), F32),
             pltpu.VMEM((1024, K), F32),
             pltpu.VMEM((K, K), F32),
             pltpu.VMEM((7, 16, K), F32),
@@ -392,7 +427,8 @@
             pltpu.VMEM((64, K), F32),
             pltpu.VMEM((64, K), F32),
             dma((2, 4)),
-            dma((7,)), dma((7,)), dma((7,)), dma((7,)), dma((7,)), dma((7,)), dma((7,)), dma((7,)),
+            dma((2, 7)), dma((2, 7)), dma((2, 7)), dma((2, 7)),
+            dma((2, 7)), dma((2, 7)), dma((2, 7)), dma((2, 7)),
             dma((7,)), dma((7,)), dma((7,)), dma((7,)), dma((7,)), dma((7,)), dma((4,)), dma((4,)),
             dma((7,)), dma((7,)), dma((7,)), dma((7,)),
         ],

time: 404 us -> 335 us (0.83)
  Pallas kernels: 396 us -> 328 us
    pallas_call x1, Pallas kernels: 396 us -> 328 us  [local(): pl.pallas_call(kernel, out_shape=(jax.ShapeDtypeStruct((1024, K), F32), j...]
where the time goes in v2:
time: 335 us
  Pallas kernels  328 us (98%)
  local copies, waits for them, and re-layouts  6.57 us (2%)
    pallas_call x1, Pallas kernels, local(): pl.pallas_call(kernel, out_shape=(jax.ShapeDtypeStruct((1024, K), F32), j...  328 us

profile of v2, /device:TPU:1, one launch (start us, length us, event | category | flops | bytes accessed | tf_op | source)
XLA Modules:
  0.0 334.9 jit_solution(17474611437476880524)
XLA Ops:
  0.6 0.0 copy-start
  0.6 1.6 copy-done
  2.2 0.0 copy-start.1
  2.2 1.0 copy-done.1
  3.3 0.0 copy-start.2
  3.3 1.0 copy-done.2
  4.3 0.0 copy-start.3
  4.3 0.7 copy-done.3
  5.0 327.7 %subspace.1 = (f32[1024,128]{1,0:T(8,128)S(1)}, f32[1024,128]{1,0:T(8,128)S(1)}, f32[128,128]{1,0:T(8,128)S(1)}) custom-call(bf16[1024,1024]{1,0:T(8,128)(2,1)S(1)} %copy-done, bf16[1024,1024]{1,0:T(8,128)(2,1)} %grad_ref.1, f32[1024,128]{1,0:T(8,128)S(1)} %copy-done.1, f32[1024,128]{1,0:T(8,128)S(1)} %copy-done.2, s32[8,128]{1,0:T(8,128)S(1)} %bitcast.1), custom_call_target="tpu_custom_call" | custom-call | tf_op jit(solution)/shard_map/subspace/pallas_call | solution.py:392
  332.7 0.8 copy.11
  333.5 0.8 copy.12
  334.3 0.6 copy.13
Async XLA Ops:
  0.6 1.6 copy-start
  2.2 1.0 copy-start.1
  3.3 1.0 copy-start.2
  4.3 0.7 copy-start.3

commit v3 on v2

--- a/solution.py
+++ b/solution.py
@@ -19,14 +19,12 @@
 
 def pieces(value):
     high = value.astype(BF16)
-    rest = value - high.astype(F32)
-    mid = rest.astype(BF16)
-    low = (rest - mid.astype(F32)).astype(BF16)
-    return jnp.concatenate([high, mid, low], axis=1)
+    low = (value - high.astype(F32)).astype(BF16)
+    return jnp.concatenate([high, low], axis=1)
 
 
 def joined(product):
-    return product[:, :K] + (product[:, K : 2 * K] + product[:, 2 * K :])
+    return product[:, :K] + product[:, K:]
 
 
 def times(a, b):
@@ -102,9 +100,8 @@
     pl.semaphore_wait(barrier, 15)
 
     even = core == 0
-    ids_own = pl.ds(pl.multiple_of(core * 8, 8), 8)
-    ids[ids_own, :] = ids_ref[...]
-    ids_copy = to_core(0, ids.at[ids_own, :], ids.at[ids_own, :])
+    ids[:8, :] = ids_ref[...]
+    ids_copy = to_core(0, ids.at[:8, :], ids.at[8:, :])
     ids_copy.start()
     x_copies = []
     for i in range(4):
@@ -119,43 +116,32 @@
         x_copies.append(copy)
     for i in range(4):
         rows = slice(i * 256, (i + 1) * 256)
-        x[pl.ds(pl.multiple_of(core * 1024 + i * 256, 256), 256), :] = jnp.where(
+        x[rows, :] = jnp.where(
             even, act_ref[rows, :].astype(F32), grad_ref[rows, :].astype(F32)
         ).astype(BF16)
     v[...] = jnp.where(even, start_act_ref[...], start_grad_ref[...])
     lane = lax.broadcasted_iota(jnp.int32, (K, K), 1)
     row = lax.broadcasted_iota(jnp.int32, (K, K), 0)
     inverse[...] = (lane == row).astype(F32)
-    for i in range(4):
-        x_copies[i].wait()
-        x[pl.ds(pl.multiple_of((1 - core) * 1024 + i * 256, 256), 256), :] = x_recv[
-            i * 256 : (i + 1) * 256, :
-        ].astype(BF16)
-
-    def token_rows(f):
-        return pl.ds(pl.multiple_of(f * 256, 256), 256)
+    def half_rows(f, h):
+        return pl.ds(pl.multiple_of(h * 1024 + f * 128, 128), 128)
+
+    def pair_rows(j, h):
+        return pl.ds(pl.multiple_of(h * 1024 + j * 256, 256), 256)
 
     def gram_rows(f):
         return pl.ds(pl.multiple_of(f * 16, 16), 16)
-
-    def half_rows(f, h):
-        return pl.ds(pl.multiple_of(f * 256 + h * 128, 128), 128)
 
     def y_copy(r, h):
         return to_feat(
             r, y_send.at[half_rows(feat_peer(r), h), :], y_recv.at[r, h], y_ssem.at[h], y_rsem.at[h]
         )
 
-    def project():
-        split[...] = pieces(v[...])
-        for r in range(7):
-            rows = token_rows(feat_peer(r))
-            y_send[rows, :] = joined(times(x[rows, :], split[...]))
-            y_copy(r, 0).start()
-        for r in range(7):
-            y_copy(r, 1).start()
-        rows = token_rows(feat)
+    def project_half(h):
+        rows = slice(h * 1024, (h + 1) * 1024)
         y_send[rows, :] = joined(times(x[rows, :], split[...]))
+        for r in range(7):
+            y_copy(r, h).start()
 
     def projected(h):
         for r in range(7):
@@ -168,12 +154,8 @@
     def gram_send():
         image = v[...]
         g_send[...] = full(image, image, (0, 0))
-        copies = []
-        for r in range(7):
-            copy = to_feat(r, g_send.at[gram_rows(feat_peer(r)), :], g_recv.at[r], gs_ssem, gs_rsem)
+        for copy in gram_copies():
             copy.start()
-            copies.append(copy)
-        return copies
 
     def gram_copies():
         return [
@@ -228,10 +210,10 @@
             copy.wait()
         work[:, :K] = g[...]
         work[:, K:] = (lane == row).astype(F32)
-        eliminate(0, 8)
+        eliminate(0, 5)
 
     def factor_end():
-        eliminate(8, 16)
+        eliminate(5, 16)
         inverse[...] = work[:, K:]
 
     def p_copy(r, h):
@@ -249,54 +231,67 @@
     def part_rows(i, h):
         return pl.ds(pl.multiple_of(i * 128 + h * 64, 64), 64)
 
+    def c_copy(r):
+        return to_dp(r, c_recv.at[q], c_recv.at[q], c_ssem, c_rsem)
+
+    def count_documents():
+        ids_copy.wait()
+        counts = jnp.zeros((1, K), F32)
+        for i in range(16):
+            column = jnp.broadcast_to(ids[i : i + 1, :].astype(F32), (K, K)).T
+            counts = counts + jnp.sum((column == lane.astype(F32)).astype(F32), axis=0, keepdims=True)
+        c_recv[q] = jnp.broadcast_to(counts, (8, K))
+        for r in range(7):
+            c_copy(r).start()
+
+    def receive_rest():
+        for i in range(4):
+            x_copies[i].wait()
+            x[1024 + i * 256 : 1280 + i * 256, :] = x_recv[i * 256 : (i + 1) * 256, :].astype(BF16)
+
+    def transpose():
+        for c in range(8):
+            xt[c] = x[c * 256 : (c + 1) * 256, :].T
+
     def sweep(step, _):
-        project()
-
-        @pl.when(step > 0)
-        def _():
-            gram_send()
+        split[...] = pieces(v[...])
+        project_half(0)
+        pl.when(step == 0)(receive_rest)
+        project_half(1)
+        pl.when(step > 0)(gram_send)
 
         @pl.when(step == 0)
         def _():
-            for c in range(16):
-                xt[c] = x[c * 128 : (c + 1) * 128, :].T
+            transpose()
+            count_documents()
 
         p[half_rows(feat, 0), :] = projected(0)
-
-        @pl.when(step > 0)
-        def _():
-            gram_sum()
-
         for r in range(7):
             p_copy(r, 0).start()
+        pl.when(step > 0)(gram_sum)
         p[half_rows(feat, 1), :] = projected(1)
         for r in range(7):
             p_copy(r, 1).start()
 
-        @pl.when(step > 0)
-        def _():
-            factor_start()
-
         for h in range(2):
-            part = joined(times(xt[feat * 2 + h], pieces(p[half_rows(feat, h), :])))
+            for dz in (0, 1, 3, 2):
+                for r in range(7):
+                    if OFFSETS[r][0] == dz:
+                        p_copy(r, h).wait()
+                j = (fz + 4 - dz) % 4
+                part = joined(times(xt[h * 4 + j], pieces(p[pair_rows(j, h), :])))
+                if h == 0 and dz == 0:
+                    v_send[...] = part
+                else:
+                    v_send[...] += part
             if h == 0:
-                v_send[...] = part
-            else:
-                v_send[...] += part
-            for r in reversed(range(7)):
-                p_copy(r, h).wait()
-                source = feat_from(r)
-                v_send[...] += joined(
-                    times(xt[source * 2 + h], pieces(p[half_rows(source, h), :]))
-                )
+                pl.when(step > 0)(factor_start)
 
         for h in range(2):
             for r in range(7):
                 v_copy(r, h).start()
 
-        @pl.when(step > 0)
-        def _():
-            factor_end()
+        pl.when(step > 0)(factor_end)
 
         for h in range(2):
             for r in range(7):
@@ -314,30 +309,13 @@
 
     lax.fori_loop(0, ITERS, sweep, 0)
 
-    project()
     gram_send()
-    ids_copy.wait()
-    counts = jnp.zeros((1, K), F32)
-    for i in range(16):
-        column = jnp.broadcast_to(ids[i : i + 1, :].astype(F32), (K, K)).T
-        counts = counts + jnp.sum((column == lane.astype(F32)).astype(F32), axis=0, keepdims=True)
-    c_recv[q] = jnp.broadcast_to(counts, (8, K))
-    c_copies = [to_dp(r, c_recv.at[q], c_recv.at[q], c_ssem, c_rsem) for r in range(7)]
-    for copy in c_copies:
-        copy.start()
-
+    split[...] = pieces(v[...])
+    project_half(0)
+    project_half(1)
     gram_sum()
-    total = jnp.concatenate([projected(0), projected(1)], axis=0)
-    factor_start()
-    factor_end()
-    basis_mine[...] = full(v[...], inverse[...], (1, 1))
-    proj_mine[...] = full(total, inverse[...], (1, 1))
-    proj_copy = to_core(1, proj_mine, proj_other)
-    proj_copy.start()
-    basis_copy = to_core(2, basis_mine, basis_other)
-    basis_copy.start()
-    for copy in c_copies:
-        copy.wait()
+    for r in range(7):
+        c_copy(r).wait()
     counts = c_recv[0]
     for i in range(1, 8):
         counts = counts + c_recv[i]
@@ -346,11 +324,25 @@
     share = jnp.where(counts > 0, 1.0 / (documents * jnp.maximum(counts, 1.0)), 0.0)
     weight = []
     for i in range(2):
-        column = jnp.broadcast_to(ids[pl.ds(feat * 2 + i, 1), :].astype(F32), (K, K)).T
+        column = jnp.broadcast_to(ids[pl.ds(i * 8 + feat, 1), :].astype(F32), (K, K)).T
         weight.append(
             jnp.sum(jnp.where(column == lane.astype(F32), share, 0.0), axis=1, keepdims=True)
         )
-    proj_copy.wait()
+    factor_start()
+    factor_end()
+    total = jnp.concatenate([projected(0), projected(1)], axis=0)
+    proj_mine[...] = full(total, inverse[...], (1, 1))
+    proj_copies = [
+        to_core(i, proj_mine.at[mine, :], proj_other.at[theirs, :])
+        for i, mine, theirs in ((1, slice(0, 128), slice(128, 256)), (4, slice(128, 256), slice(0, 128)))
+    ]
+    for copy in proj_copies:
+        copy.start()
+    basis_mine[...] = full(v[...], inverse[...], (1, 1))
+    basis_copy = to_core(2, basis_mine, basis_other)
+    basis_copy.start()
+    for copy in proj_copies:
+        copy.wait()
     proj_act = jnp.where(even, proj_mine[...], proj_other[...])
     proj_grad = jnp.where(even, proj_other[...], proj_mine[...])
     left = jnp.concatenate(weight, axis=0) * proj_grad * proj_grad
@@ -402,8 +394,8 @@
             pltpu.VMEM((1024, 1024), F32),
             pltpu.VMEM((1024, 1024), F32),
             pltpu.VMEM((2048, 1024), BF16),
-            pltpu.VMEM((16, 1024, 128), BF16),
-            pltpu.VMEM((1024, 3 * K), BF16),
+            pltpu.VMEM((8, 1024, 256), BF16),
+            pltpu.VMEM((1024, 2 * K), BF16),
             pltpu.VMEM((2048, K), F32),
             pltpu.VMEM((7, 2, 128, K), F32),
             pltpu.VMEM((2048, K), F32),
@@ -429,7 +421,7 @@
             dma((2, 4)),
             dma((2, 7)), dma((2, 7)), dma((2, 7)), dma((2, 7)),
             dma((2, 7)), dma((2, 7)), dma((2, 7)), dma((2, 7)),
-            dma((7,)), dma((7,)), dma((7,)), dma((7,)), dma((7,)), dma((7,)), dma((4,)), dma((4,)),
+            dma((7,)), dma((7,)), dma((7,)), dma((7,)), dma((7,)), dma((7,)), dma((5,)), dma((5,)),
             dma((7,)), dma((7,)), dma((7,)), dma((7,)),
         ],
         compiler_params=pltpu.CompilerParams(

time: 335 us -> 310 us (0.925)
  Pallas kernels: 328 us -> 302 us
    pallas_call x1, Pallas kernels: 328 us -> 302 us  [local(): pl.pallas_call(kernel, out_shape=(jax.ShapeDtypeStruct((1024, K), F32), j...]
where the time goes in v3:
time: 310 us; the launch traced here: 309 us
  Pallas kernels  302 us (97%)
  local copies, waits for them, and re-layouts  6.57 us (2%)
    pallas_call x1, Pallas kernels, local(): pl.pallas_call(kernel, out_shape=(jax.ShapeDtypeStruct((1024, K), F32), j...  302 us
    unnamed x11, local copies, waits for them, and re-layouts  6.57 us

profile of v3, /device:TPU:1, one launch (start us, length us, event | category | flops | bytes accessed | tf_op | source)
XLA Modules:
  0.0 309.2 jit_solution(11645832748670279954)
XLA Ops:
  0.6 0.0 copy-start
  0.6 1.6 copy-done
  2.2 0.0 copy-start.1
  2.2 1.0 copy-done.1
  3.3 0.0 copy-start.2
  3.3 1.0 copy-done.2
  4.3 0.0 copy-start.3
  4.3 0.7 copy-done.3
  5.0 302.0 %subspace.1 = (f32[1024,128]{1,0:T(8,128)S(1)}, f32[1024,128]{1,0:T(8,128)S(1)}, f32[128,128]{1,0:T(8,128)S(1)}) custom-call(bf16[1024,1024]{1,0:T(8,128)(2,1)S(1)} %copy-done, bf16[1024,1024]{1,0:T(8,128)(2,1)} %grad_ref.1, f32[1024,128]{1,0:T(8,128)S(1)} %copy-done.1, f32[1024,128]{1,0:T(8,128)S(1)} %copy-done.2, s32[8,128]{1,0:T(8,128)S(1)} %bitcast.1), custom_call_target="tpu_custom_call" | custom-call | tf_op jit(solution)/shard_map/subspace/pallas_call | solution.py:384
  307.0 0.8 copy.11
  307.8 0.8 copy.12
  308.6 0.6 copy.13
Async XLA Ops:
  0.6 1.6 copy-start
  2.2 1.0 copy-start.1
  3.3 1.0 copy-start.2
  4.3 0.7 copy-start.3

commit v4 on v3

--- a/solution.py
+++ b/solution.py
@@ -8,6 +8,7 @@
 from jax.sharding import PartitionSpec as P
 
 ITERS = 6
+FIRST, SECOND = 6, 11
 K = 128
 MESH = pl.DeviceIdType.MESH
 F32 = jnp.float32
@@ -40,13 +41,13 @@
 def kernel(
     act_ref, grad_ref, start_act_ref, start_grad_ref, ids_ref,
     basis_act_ref, basis_grad_ref, scales_ref,
-    x_send, x_recv, x, xt, split,
+    x_stage, x_send, x_recv, x, xt, split,
     y_send, y_recv, p, v_send, v_recv, v,
-    g_send, g_recv, g, work, inverse,
+    g_send, g_recv, g_feat, g, work, inverse,
     ids, c_recv, proj_mine, proj_other, basis_mine, basis_other,
     s_part, s_feat, s_dp, s_mine, s_other,
-    x_sems, y_ssem, y_rsem, p_ssem, p_rsem, v_ssem, v_rsem, w_ssem, w_rsem,
-    gs_ssem, gs_rsem, ga_ssem, ga_rsem, c_ssem, c_rsem, core_ssem, core_rsem,
+    load_sems, x_sems, y_ssem, y_rsem, p_ssem, p_rsem, v_ssem, v_rsem, w_ssem, w_rsem,
+    gs_ssem, gs_rsem, gf_ssem, gf_rsem, ga_ssem, ga_rsem, c_ssem, c_rsem, core_ssem, core_rsem,
     sf_ssem, sf_rsem, sd_ssem, sd_rsem,
 ):
     dp, feat = lax.axis_index("dp"), lax.axis_index("feat")
@@ -97,16 +98,40 @@
     pl.semaphore_signal(
         barrier, inc=1, device_id={"dp": q * 2 + (1 - core)}, device_id_type=MESH
     )
+
+    even = core == 0
+
+    def load(mine, theirs, start):
+        own = [
+            pltpu.make_async_copy(start, v, load_sems.at[0]),
+            pltpu.make_async_copy(mine, x.at[:1024, :], load_sems.at[1]),
+        ]
+        other = [
+            pltpu.make_async_copy(
+                theirs.at[i * 256 : (i + 1) * 256, :],
+                x_stage.at[i * 256 : (i + 1) * 256, :],
+                load_sems.at[2 + i],
+            )
+            for i in range(4)
+        ]
+        for copy in other + own:
+            copy.start()
+        for i in range(4):
+            rows = slice(i * 256, (i + 1) * 256)
+            other[i].wait()
+            x_send[rows, :] = x_stage[rows, :].astype(F32)
+        for copy in own:
+            copy.wait()
+
+    pl.when(even)(lambda: load(act_ref, grad_ref, start_act_ref))
+    pl.when(core == 1)(lambda: load(grad_ref, act_ref, start_grad_ref))
+    ids[:8, :] = ids_ref[...]
     pl.semaphore_wait(barrier, 15)
-
-    even = core == 0
-    ids[:8, :] = ids_ref[...]
     ids_copy = to_core(0, ids.at[:8, :], ids.at[8:, :])
     ids_copy.start()
     x_copies = []
     for i in range(4):
         rows = slice(i * 256, (i + 1) * 256)
-        x_send[rows, :] = jnp.where(even, grad_ref[rows, :].astype(F32), act_ref[rows, :].astype(F32))
         copy = pltpu.make_async_remote_copy(
             src_ref=x_send.at[rows, :], dst_ref=x_recv.at[rows, :],
             send_sem=x_sems.at[0, i], recv_sem=x_sems.at[1, i],
@@ -114,12 +139,6 @@
         )
         copy.start()
         x_copies.append(copy)
-    for i in range(4):
-        rows = slice(i * 256, (i + 1) * 256)
-        x[rows, :] = jnp.where(
-            even, act_ref[rows, :].astype(F32), grad_ref[rows, :].astype(F32)
-        ).astype(BF16)
-    v[...] = jnp.where(even, start_act_ref[...], start_grad_ref[...])
     lane = lax.broadcasted_iota(jnp.int32, (K, K), 1)
     row = lax.broadcasted_iota(jnp.int32, (K, K), 0)
     inverse[...] = (lane == row).astype(F32)
@@ -129,19 +148,22 @@
     def pair_rows(j, h):
         return pl.ds(pl.multiple_of(h * 1024 + j * 256, 256), 256)
 
-    def gram_rows(f):
-        return pl.ds(pl.multiple_of(f * 16, 16), 16)
+    def gram_rows(i):
+        return pl.ds(pl.multiple_of(i * 16, 16), 16)
 
     def y_copy(r, h):
         return to_feat(
             r, y_send.at[half_rows(feat_peer(r), h), :], y_recv.at[r, h], y_ssem.at[h], y_rsem.at[h]
         )
 
-    def project_half(h):
-        rows = slice(h * 1024, (h + 1) * 1024)
-        y_send[rows, :] = joined(times(x[rows, :], split[...]))
-        for r in range(7):
-            y_copy(r, h).start()
+    def project_half(h, send):
+        for dz in (2, 1, 3, 0):
+            rows = pair_rows((fz + dz) % 4, h)
+            y_send[rows, :] = joined(times(x[rows, :], split[...]))
+            if send:
+                for r in range(7):
+                    if OFFSETS[r][0] == dz:
+                        y_copy(r, h).start()
 
     def projected(h):
         for r in range(7):
@@ -151,29 +173,42 @@
             total = total + y_recv[r, h]
         return total
 
-    def gram_send():
-        image = v[...]
-        g_send[...] = full(image, image, (0, 0))
-        for copy in gram_copies():
-            copy.start()
-
-    def gram_copies():
+    def gram_scatters():
         return [
-            to_feat(r, g_send.at[gram_rows(feat_peer(r)), :], g_recv.at[r], gs_ssem, gs_rsem)
+            to_dp(r, g_send.at[gram_rows(q_peer(r)), :], g_recv.at[r], gs_ssem, gs_rsem)
             for r in range(7)
         ]
 
+    def gram_swaps():
+        return [to_feat(r, g_feat.at[feat], g_feat.at[feat], gf_ssem, gf_rsem) for r in range(7)]
+
     def gram_gathers():
-        mine = gram_rows(feat)
-        return [to_feat(r, g.at[mine, :], g.at[mine, :], ga_ssem, ga_rsem) for r in range(7)]
-
-    def gram_sum():
-        for copy in gram_copies():
+        mine = gram_rows(q)
+        return [to_dp(r, g.at[mine, :], g.at[mine, :], ga_ssem, ga_rsem) for r in range(7)]
+
+    def gram_scatter():
+        piece = v[pl.ds(pl.multiple_of(q * 128, 128), 128), :]
+        g_send[...] = full(piece, piece, (0, 0))
+        for copy in gram_scatters():
+            copy.start()
+
+    def gram_swap():
+        for copy in gram_scatters():
             copy.wait()
-        total = g_send[gram_rows(feat), :]
+        total = g_send[gram_rows(q), :]
         for r in range(7):
             total = total + g_recv[r]
-        g[gram_rows(feat), :] = total
+        g_feat[feat] = total
+        for copy in gram_swaps():
+            copy.start()
+
+    def gram_gather():
+        for copy in gram_swaps():
+            copy.wait()
+        total = g_feat[0]
+        for i in range(1, 8):
+            total = total + g_feat[i]
+        g[gram_rows(q), :] = total
         for copy in gram_gathers():
             copy.start()
 
@@ -210,10 +245,13 @@
             copy.wait()
         work[:, :K] = g[...]
         work[:, K:] = (lane == row).astype(F32)
-        eliminate(0, 5)
+        eliminate(0, FIRST)
+
+    def factor_middle():
+        eliminate(FIRST, SECOND)
 
     def factor_end():
-        eliminate(5, 16)
+        eliminate(SECOND, 16)
         inverse[...] = work[:, K:]
 
     def p_copy(r, h):
@@ -255,10 +293,10 @@
 
     def sweep(step, _):
         split[...] = pieces(v[...])
-        project_half(0)
+        project_half(0, True)
         pl.when(step == 0)(receive_rest)
-        project_half(1)
-        pl.when(step > 0)(gram_send)
+        project_half(1, True)
+        pl.when(step > 0)(gram_gather)
 
         @pl.when(step == 0)
         def _():
@@ -268,11 +306,11 @@
         p[half_rows(feat, 0), :] = projected(0)
         for r in range(7):
             p_copy(r, 0).start()
-        pl.when(step > 0)(gram_sum)
         p[half_rows(feat, 1), :] = projected(1)
         for r in range(7):
             p_copy(r, 1).start()
 
+        pl.when(step > 0)(factor_start)
         for h in range(2):
             for dz in (0, 1, 3, 2):
                 for r in range(7):
@@ -285,7 +323,7 @@
                 else:
                     v_send[...] += part
             if h == 0:
-                pl.when(step > 0)(factor_start)
+                pl.when(step > 0)(factor_middle)
 
         for h in range(2):
             for r in range(7):
@@ -302,18 +340,21 @@
             v[part_rows(q, h), :] = full(total, inverse[...], (1, 1))
             for r in range(7):
                 w_copy(r, h).start()
+        gram_scatter()
         for h in range(2):
             for r in range(7):
                 w_copy(r, h).wait()
+        gram_swap()
         return 0
 
     lax.fori_loop(0, ITERS, sweep, 0)
 
-    gram_send()
     split[...] = pieces(v[...])
-    project_half(0)
-    project_half(1)
-    gram_sum()
+    project_half(0, True)
+    project_half(1, False)
+    gram_gather()
+    for r in range(7):
+        y_copy(r, 1).start()
     for r in range(7):
         c_copy(r).wait()
     counts = c_recv[0]
@@ -329,6 +370,7 @@
             jnp.sum(jnp.where(column == lane.astype(F32), share, 0.0), axis=1, keepdims=True)
         )
     factor_start()
+    factor_middle()
     factor_end()
     total = jnp.concatenate([projected(0), projected(1)], axis=0)
     proj_mine[...] = full(total, inverse[...], (1, 1))
@@ -380,6 +422,7 @@
 
 def local(activations, gradients, start_act, start_grad, doc_ids):
     vmem = pl.BlockSpec(memory_space=pltpu.VMEM)
+    hbm = pl.BlockSpec(memory_space=pl.ANY)
     dma = pltpu.SemaphoreType.DMA
     return pl.pallas_call(
         kernel,
@@ -388,9 +431,10 @@
             jax.ShapeDtypeStruct((1024, K), F32),
             jax.ShapeDtypeStruct((K, K), F32),
         ),
-        in_specs=[vmem] * 5,
+        in_specs=[hbm] * 4 + [vmem],
         out_specs=(vmem,) * 3,
         scratch_shapes=[
+            pltpu.VMEM((1024, 1024), BF16),
             pltpu.VMEM((1024, 1024), F32),
             pltpu.VMEM((1024, 1024), F32),
             pltpu.VMEM((2048, 1024), BF16),
@@ -404,6 +448,7 @@
             pltpu.VMEM((1024, K), F32),
             pltpu.VMEM((K, K), F32),
             pltpu.VMEM((7, 16, K), F32),
+            pltpu.VMEM((8, 16, K), F32),
             pltpu.VMEM((K, K), F32),
             pltpu.VMEM((K, 2 * K), F32),
             pltpu.VMEM((K, K), F32),
@@ -418,14 +463,15 @@
             pltpu.VMEM((8, 64, K), F32),
             pltpu.VMEM((64, K), F32),
             pltpu.VMEM((64, K), F32),
-            dma((2, 4)),
+            dma((6,)), dma((2, 4)),
             dma((2, 7)), dma((2, 7)), dma((2, 7)), dma((2, 7)),
             dma((2, 7)), dma((2, 7)), dma((2, 7)), dma((2, 7)),
-            dma((7,)), dma((7,)), dma((7,)), dma((7,)), dma((7,)), dma((7,)), dma((5,)), dma((5,)),
+            dma((7,)), dma((7,)), dma((7,)), dma((7,)), dma((7,)), dma((7,)), dma((7,)), dma((7,)),
+            dma((5,)), dma((5,)),
             dma((7,)), dma((7,)), dma((7,)), dma((7,)),
         ],
         compiler_params=pltpu.CompilerParams(
-            collective_id=0, has_side_effects=True, vmem_limit_bytes=48 * 2**20
+            collective_id=0, has_side_effects=True, vmem_limit_bytes=60 * 2**20
         ),
         name="subspace",
     )(activations, gradients, start_act, start_grad, doc_ids.reshape(8, 128))

time: 310 us -> 296 us (0.955)
  Pallas kernels: 302 us -> 291 us
    pallas_call x1, Pallas kernels: 302 us -> 291 us  [local(): pl.pallas_call(kernel, out_shape=(jax.ShapeDtypeStruct((1024, K), F32), j...]
    unnamed x11 -> x5, local copies, waits for them, and re-layouts: 6.57 us -> 4.4 us
where the time goes in v4:
time: 296 us
  Pallas kernels  291 us (98%)
  local copies, waits for them, and re-layouts  4.4 us (1%)
    pallas_call x1, Pallas kernels, local(): pl.pallas_call(kernel, out_shape=(jax.ShapeDtypeStruct((1024, K), F32), j...  291 us

profile of v4, /device:TPU:1, one launch (start us, length us, event | category | flops | bytes accessed | tf_op | source)
XLA Modules:
  0.0 295.7 jit_solution(10793948540138004389)
XLA Ops:
  0.6 290.7 %subspace.1 = (f32[1024,128]{1,0:T(8,128)}, f32[1024,128]{1,0:T(8,128)}, f32[128,128]{1,0:T(8,128)}) custom-call(bf16[1024,1024]{1,0:T(8,128)(2,1)} %act_ref.1, bf16[1024,1024]{1,0:T(8,128)(2,1)} %grad_ref.1, f32[1024,128]{1,0:T(8,128)} %start_act_ref.1, f32[1024,128]{1,0:T(8,128)} %start_grad_ref.1, s32[8,128]{1,0:T(8,128)} %bitcast.1), custom_call_target="tpu_custom_call" | custom-call | tf_op jit(solution)/shard_map/subspace/pallas_call | solution.py:427
  291.3 0.0 copy-start
  291.3 1.9 copy.11
  293.2 1.9 copy.12
  295.1 0.0 copy-done
  295.1 0.6 copy.13
Async XLA Ops:
  291.3 3.8 %copy-start = (f32[128,128]{1,0:T(8,128)S(1)}, f32[128,128]{1,0:T(8,128)}, u32[]{:S(2)}) copy-start(f32[128,128]{1,0:T(8,128)} %get-tuple-element.8) | copy-start | bytes 196612

commit v5 on v4

--- a/solution.py
+++ b/solution.py
@@ -8,7 +8,7 @@
 from jax.sharding import PartitionSpec as P
 
 ITERS = 6
-FIRST, SECOND = 6, 11
+FIRST, SECOND = 3, 5
 K = 128
 MESH = pl.DeviceIdType.MESH
 F32 = jnp.float32
@@ -48,7 +48,7 @@
     s_part, s_feat, s_dp, s_mine, s_other,
     load_sems, x_sems, y_ssem, y_rsem, p_ssem, p_rsem, v_ssem, v_rsem, w_ssem, w_rsem,
     gs_ssem, gs_rsem, gf_ssem, gf_rsem, ga_ssem, ga_rsem, c_ssem, c_rsem, core_ssem, core_rsem,
-    sf_ssem, sf_rsem, sd_ssem, sd_rsem,
+    sf_ssem, sf_rsem, sd_ssem, sd_rsem, late_sem,
 ):
     dp, feat = lax.axis_index("dp"), lax.axis_index("feat")
     core, q = dp % 2, dp // 2
@@ -213,20 +213,20 @@
             copy.start()
 
     def eliminate(first, last):
-        small_row = lax.broadcasted_iota(jnp.int32, (8, K), 0)
+        small_row = lax.broadcasted_iota(jnp.int32, (16, K), 0)
         wide_row = lax.broadcasted_iota(jnp.int32, (K, 2 * K), 0)
 
         def panel(i, _):
-            at = pl.ds(pl.multiple_of(i * 8, 8), 8)
+            at = pl.ds(pl.multiple_of(i * 16, 16), 16)
             left, right = work[at, :K], work[at, K:]
-            block = pltpu.roll(left, (K - i * 8) % K, 1)
-            column = [jnp.broadcast_to(block[:, j : j + 1], (8, K)) for j in range(8)]
-            pivots = jnp.ones((8, K), F32)
-            for j in range(8):
-                pivot = jnp.broadcast_to(column[j][j : j + 1, :], (8, K))
+            block = pltpu.roll(left, (K - i * 16) % K, 1)
+            column = [jnp.broadcast_to(block[:, j : j + 1], (16, K)) for j in range(16)]
+            pivots = jnp.ones((16, K), F32)
+            for j in range(16):
+                pivot = jnp.broadcast_to(column[j][j : j + 1, :], (16, K))
                 ratio = jnp.where(small_row > j, column[j] * (1.0 / pivot), 0.0)
                 pivots = jnp.where(small_row == j, pivot, pivots)
-                for k in range(j + 1, 8):
+                for k in range(j + 1, 16):
                     column[k] = column[k] - ratio * column[k][j : j + 1, :]
                 left = left - ratio * left[j : j + 1, :]
                 right = right - ratio * right[j : j + 1, :]
@@ -234,7 +234,7 @@
             scale = scale * (1.5 - 0.5 * pivots * scale * scale)
             fresh = jnp.concatenate([left * scale, right * scale], axis=1)
             update = full(fresh[:, :K], fresh, (0, 0))
-            work[...] = jnp.where(wide_row >= i * 8 + 8, work[...] - update, work[...])
+            work[...] = jnp.where(wide_row >= i * 16 + 16, work[...] - update, work[...])
             work[at, :] = fresh
             return 0
 
@@ -251,7 +251,7 @@
         eliminate(FIRST, SECOND)
 
     def factor_end():
-        eliminate(SECOND, 16)
+        eliminate(SECOND, 8)
         inverse[...] = work[:, K:]
 
     def p_copy(r, h):
@@ -287,21 +287,26 @@
             x_copies[i].wait()
             x[1024 + i * 256 : 1280 + i * 256, :] = x_recv[i * 256 : (i + 1) * 256, :].astype(BF16)
 
-    def transpose():
-        for c in range(8):
+    def transpose(h):
+        for c in range(4 * h, 4 * h + 4):
             xt[c] = x[c * 256 : (c + 1) * 256, :].T
 
     def sweep(step, _):
         split[...] = pieces(v[...])
+
+        @pl.when((step == 0) & (core == 1))
+        def _():
+            pl.semaphore_wait(late_sem, 1)
+
         project_half(0, True)
-        pl.when(step == 0)(receive_rest)
+
+        @pl.when(step == 0)
+        def _():
+            transpose(0)
+            receive_rest()
+
         project_half(1, True)
         pl.when(step > 0)(gram_gather)
-
-        @pl.when(step == 0)
-        def _():
-            transpose()
-            count_documents()
 
         p[half_rows(feat, 0), :] = projected(0)
         for r in range(7):
@@ -311,6 +316,12 @@
             p_copy(r, 1).start()
 
         pl.when(step > 0)(factor_start)
+
+        @pl.when(step == 0)
+        def _():
+            transpose(1)
+            count_documents()
+
         for h in range(2):
             for dz in (0, 1, 3, 2):
                 for r in range(7):
@@ -324,6 +335,10 @@
                     v_send[...] += part
             if h == 0:
                 pl.when(step > 0)(factor_middle)
+
+        @pl.when((step == 0) & (core == 0))
+        def _():
+            pl.semaphore_signal(late_sem, inc=1, device_id={"dp": q * 2 + 1}, device_id_type=MESH)
 
         for h in range(2):
             for r in range(7):
@@ -380,9 +395,6 @@
     ]
     for copy in proj_copies:
         copy.start()
-    basis_mine[...] = full(v[...], inverse[...], (1, 1))
-    basis_copy = to_core(2, basis_mine, basis_other)
-    basis_copy.start()
     for copy in proj_copies:
         copy.wait()
     proj_act = jnp.where(even, proj_mine[...], proj_other[...])
@@ -395,6 +407,9 @@
     copies = [to_feat(r, s_feat.at[feat], s_feat.at[feat], sf_ssem, sf_rsem) for r in range(7)]
     for copy in copies:
         copy.start()
+    basis_mine[...] = full(v[...], inverse[...], (1, 1))
+    basis_copy = to_core(2, basis_mine, basis_other)
+    basis_copy.start()
     for copy in copies:
         copy.wait()
     total = s_feat[0]
@@ -468,7 +483,7 @@
             dma((2, 7)), dma((2, 7)), dma((2, 7)), dma((2, 7)),
             dma((7,)), dma((7,)), dma((7,)), dma((7,)), dma((7,)), dma((7,)), dma((7,)), dma((7,)),
             dma((5,)), dma((5,)),
-            dma((7,)), dma((7,)), dma((7,)), dma((7,)),
+            dma((7,)), dma((7,)), dma((7,)), dma((7,)), pltpu.SemaphoreType.REGULAR,
         ],
         compiler_params=pltpu.CompilerParams(
             collective_id=0, has_side_effects=True, vmem_limit_bytes=60 * 2**20

time: 296 us -> 285 us (0.963)
  Pallas kernels: 291 us -> 280 us
    pallas_call x1, Pallas kernels: 291 us -> 280 us  [local(): pl.pallas_call(kernel, out_shape=(jax.ShapeDtypeStruct((1024, K), F32), j...]
where the time goes in v5:
time: 285 us
  Pallas kernels  280 us (98%)
  local copies, waits for them, and re-layouts  4.4 us (2%)
    pallas_call x1, Pallas kernels, local(): pl.pallas_call(kernel, out_shape=(jax.ShapeDtypeStruct((1024, K), F32), j...  280 us

profile of v5, /device:TPU:1, one launch (start us, length us, event | category | flops | bytes accessed | tf_op | source)
XLA Modules:
  0.0 284.7 jit_solution(14929215076633064161)
XLA Ops:
  0.6 279.6 %subspace.1 = (f32[1024,128]{1,0:T(8,128)}, f32[1024,128]{1,0:T(8,128)}, f32[128,128]{1,0:T(8,128)}) custom-call(bf16[1024,1024]{1,0:T(8,128)(2,1)} %act_ref.1, bf16[1024,1024]{1,0:T(8,128)(2,1)} %grad_ref.1, f32[1024,128]{1,0:T(8,128)} %start_act_ref.1, f32[1024,128]{1,0:T(8,128)} %start_grad_ref.1, s32[8,128]{1,0:T(8,128)} %bitcast.1), custom_call_target="tpu_custom_call" | custom-call | tf_op jit(solution)/shard_map/subspace/pallas_call | solution.py:442
  280.2 0.0 copy-start
  280.2 1.9 copy.11
  282.1 1.9 copy.12
  284.0 0.0 copy-done
  284.0 0.6 copy.13
Async XLA Ops:
  280.2 3.8 %copy-start = (f32[128,128]{1,0:T(8,128)S(1)}, f32[128,128]{1,0:T(8,128)}, u32[]{:S(2)}) copy-start(f32[128,128]{1,0:T(8,128)} %get-tuple-element.8) | copy-start | bytes 196612

commit v6 on v5

--- a/solution.py
+++ b/solution.py
@@ -123,9 +123,11 @@
         for copy in own:
             copy.wait()
 
+    ids_load = pltpu.make_async_copy(ids_ref, ids.at[:8, :], load_sems.at[6])
+    ids_load.start()
     pl.when(even)(lambda: load(act_ref, grad_ref, start_act_ref))
     pl.when(core == 1)(lambda: load(grad_ref, act_ref, start_grad_ref))
-    ids[:8, :] = ids_ref[...]
+    ids_load.wait()
     pl.semaphore_wait(barrier, 15)
     ids_copy = to_core(0, ids.at[:8, :], ids.at[8:, :])
     ids_copy.start()
@@ -293,6 +295,7 @@
 
     def sweep(step, _):
         split[...] = pieces(v[...])
+        pl.when(step > 0)(gram_swap)
 
         @pl.when((step == 0) & (core == 1))
         def _():
@@ -359,12 +362,12 @@
         for h in range(2):
             for r in range(7):
                 w_copy(r, h).wait()
-        gram_swap()
         return 0
 
     lax.fori_loop(0, ITERS, sweep, 0)
 
     split[...] = pieces(v[...])
+    gram_swap()
     project_half(0, True)
     project_half(1, False)
     gram_gather()
@@ -446,7 +449,7 @@
             jax.ShapeDtypeStruct((1024, K), F32),
             jax.ShapeDtypeStruct((K, K), F32),
         ),
-        in_specs=[hbm] * 4 + [vmem],
+        in_specs=[hbm] * 5,
         out_specs=(vmem,) * 3,
         scratch_shapes=[
             pltpu.VMEM((1024, 1024), BF16),
@@ -478,7 +481,7 @@
             pltpu.VMEM((8, 64, K), F32),
             pltpu.VMEM((64, K), F32),
             pltpu.VMEM((64, K), F32),
-            dma((6,)), dma((2, 4)),
+            dma((7,)), dma((2, 4)),
             dma((2, 7)), dma((2, 7)), dma((2, 7)), dma((2, 7)),
             dma((2, 7)), dma((2, 7)), dma((2, 7)), dma((2, 7)),
             dma((7,)), dma((7,)), dma((7,)), dma((7,)), dma((7,)), dma((7,)), dma((7,)), dma((7,)),
@@ -486,7 +489,7 @@
             dma((7,)), dma((7,)), dma((7,)), dma((7,)), pltpu.SemaphoreType.REGULAR,
         ],
         compiler_params=pltpu.CompilerParams(
-            collective_id=0, has_side_effects=True, vmem_limit_bytes=60 * 2**20
+            collective_id=0, has_side_effects=True, vmem_limit_bytes=50 * 2**20
         ),
         name="subspace",
     )(activations, gradients, start_act, start_grad, doc_ids.reshape(8, 128))

time: 285 us -> 283 us (level)
  Pallas kernels: 280 us -> 277 us
where the time goes in v6:
time: 283 us
  Pallas kernels  277 us (98%)
  local copies, waits for them, and re-layouts  4.98 us (2%)
    pallas_call x1, Pallas kernels, local(): pl.pallas_call(kernel, out_shape=(jax.ShapeDtypeStruct((1024, K), F32), j...  277 us

profile of v6, /device:TPU:1, one launch (start us, length us, event | category | flops | bytes accessed | tf_op | source)
XLA Modules:
  0.0 283.0 jit_solution(151260168529986805)
XLA Ops:
  0.6 0.0 copy-start
  0.6 1.0 copy-done
  1.7 0.0 copy-start.1
  1.7 1.0 copy-done.1
  2.7 0.0 copy-start.2
  2.7 0.7 copy-done.2
  3.4 277.4 %subspace.1 = (f32[1024,128]{1,0:T(8,128)S(1)}, f32[1024,128]{1,0:T(8,128)S(1)}, f32[128,128]{1,0:T(8,128)S(1)}) custom-call(bf16[1024,1024]{1,0:T(8,128)(2,1)} %act_ref.1, bf16[1024,1024]{1,0:T(8,128)(2,1)} %grad_ref.1, f32[1024,128]{1,0:T(8,128)S(1)} %copy-done, f32[1024,128]{1,0:T(8,128)S(1)} %copy-done.1, s32[8,128]{1,0:T(8,128)S(1)} %bitcast.1), custom_call_target="tpu_custom_call" | custom-call | tf_op jit(solution)/shard_map/subspace/pallas_call | solution.py:445
  280.8 0.8 copy.11
  281.6 0.8 copy.12
  282.4 0.6 copy.13
Async XLA Ops:
  0.6 1.0 copy-start
  1.7 1.0 copy-start.1
  2.7 0.7 copy-start.2

commit v7 on v6

--- a/solution.py
+++ b/solution.py
@@ -15,7 +15,7 @@
 BF16 = jnp.bfloat16
 HIGHEST = lax.Precision.HIGHEST
 
-OFFSETS = ((2, 1), (1, 1), (3, 1), (2, 0), (0, 1), (1, 0), (3, 0))
+OFFSETS = ((2, 1), (1, 1), (3, 1), (0, 1), (2, 0), (1, 0), (3, 0))
 
 
 def pieces(value):

time: 283 us -> 284 us (level)
  no operation moved by 1% of the time
where the time goes in v7:
time: 284 us
  Pallas kernels  278 us (98%)
  local copies, waits for them, and re-layouts  4.98 us (2%)
    pallas_call x1, Pallas kernels, local(): pl.pallas_call(kernel, out_shape=(jax.ShapeDtypeStruct((1024, K), F32), j...  278 us

profile of v7, /device:TPU:1, one launch (start us, length us, event | category | flops | bytes accessed | tf_op | source)
XLA Modules:
  0.0 283.9 jit_solution(5803838565674929216)
XLA Ops:
  0.6 0.0 copy-start
  0.6 1.0 copy-done
  1.7 0.0 copy-start.1
  1.7 1.0 copy-done.1
  2.7 0.0 copy-start.2
  2.7 0.7 copy-done.2
  3.4 278.3 %subspace.1 = (f32[1024,128]{1,0:T(8,128)S(1)}, f32[1024,128]{1,0:T(8,128)S(1)}, f32[128,128]{1,0:T(8,128)S(1)}) custom-call(bf16[1024,1024]{1,0:T(8,128)(2,1)} %act_ref.1, bf16[1024,1024]{1,0:T(8,128)(2,1)} %grad_ref.1, f32[1024,128]{1,0:T(8,128)S(1)} %copy-done, f32[1024,128]{1,0:T(8,128)S(1)} %copy-done.1, s32[8,128]{1,0:T(8,128)S(1)} %bitcast.1), custom_call_target="tpu_custom_call" | custom-call | tf_op jit(solution)/shard_map/subspace/pallas_call | solution.py:445
  281.7 0.8 copy.11
  282.5 0.8 copy.12
  283.3 0.6 copy.13
Async XLA Ops:
  0.6 1.0 copy-start
  1.7 1.0 copy-start.1
  2.7 0.7 copy-start.2
